TPU v7x, 32 devices: a whole 2x2x4 slice. The times are simulated.
32 devices in a mesh: seq: 16 (over z, x, core), exp: 2 (over y).
Axes of the slice: x: 2, y: 2, z: 4, core: 2. Of those that a mesh axis runs over, the one named last changes fastest.
Arguments:
- inner_x: bfloat16 [2048, 8192], P('seq', 'exp'), may hold values from -6 to 6
- inner_z: bfloat16 [2048, 8192], P('seq', 'exp'), may hold values from -6 to 6
- step_raw: bfloat16 [2048, 8192], P('seq', 'exp'), may hold values from -4.5 to 3
- conv_weight: float32 [4, 8192], P(None, 'exp'), may hold values from -3 to 3
- state_proj: bfloat16 [8192, 32], P('exp'), may hold values from -0.125 to 0.125
- step_bias: float32 [8192], P('exp'), may hold values from -7 to -2.3
- decay_log: float32 [16, 8192], P(None, 'exp'), may hold values from -4 to 2.8
- skip_gain: float32 [8192], P('exp'), may hold values from 0.5 to 1.5
- moe_tokens: bfloat16 [2048, 4096], P('seq', 'exp'), may hold values from -6 to 6
- routes: int32 [2048, 2], P('seq'), may hold values from 0 to 15, all different within a row; in each aligned block of 128 rows (0 to 127, 128 to 255, ...) at most 20 rows name the same one
- gate_weight: bfloat16 [2, 12288, 4096], P('exp', 'seq'), may hold values from -0.09375 to 0.09375
- up_weight: bfloat16 [2, 12288, 4096], P('exp', 'seq'), may hold values from -0.09375 to 0.09375
Outputs:
- mixed: bfloat16 [2048, 8192], P('seq', 'exp')
- hidden: bfloat16 [2, 12288, 320], P('exp', 'seq')
Inputs may be any that keep to these rules, and one draw needn't show every extreme that they name: `routes`: in each aligned block of 128 rows (the tokens of one device), no expert is named by more than 20 rows, a bound that some block reaches; the two choices of a token differ.
All inputs are finite; a program needn't handle non-finite values.
Results may differ from a plain program's by a relative error of at most 0.0051.
Values may be sent and summed in bfloat16 or wider, within the bound.
A program may use at most 128 MiB of HBM per device.

v0:
```python
import jax
import jax.numpy as jnp
from jax import lax
from jax.sharding import PartitionSpec as P

CAP = 20


def from_behind(value, axis, steps):
    count = lax.axis_size(axis)
    first, last = (max(0, -steps), min(count, count - steps))
    return lax.ppermute(value, axis, [(source, source + steps) for source in range(first, last)])


def carried_in(value, axis, join, neutral):
    count, mine = (lax.axis_size(axis), lax.axis_index(axis))
    pieces = jax.tree.map(lambda part: lax.all_gather(part, axis), value)
    so_far = jax.tree.map(
        lambda part, zero: jnp.full_like(part, 0) + jnp.asarray(zero, part.dtype), value, neutral
    )

    def turn(position, so_far):
        longer = join(so_far, jax.tree.map(lambda part: part[position], pieces))
        return jax.tree.map(lambda new, old: jnp.where(position < mine, new, old), longer, so_far)

    return lax.fori_loop(0, count - 1, turn, so_far)


def pair_combine(earlier, later):
    return (earlier[0] * later[0], later[0] * earlier[1] + later[1])


def expand_rows(slot_rows, gate_matrix, up_matrix):
    dims = (((1,), (1,)), ((), ()))
    gate_part = lax.dot_general(gate_matrix, slot_rows, dims, preferred_element_type=jnp.float32)
    up_part = lax.dot_general(up_matrix, slot_rows, dims, preferred_element_type=jnp.float32)
    return (jax.nn.silu(gate_part) * up_part).astype(jnp.bfloat16)


def slot_table(pair_ids, experts_count, capacity, tokens):
    onehot = (pair_ids[:, None] == jnp.arange(experts_count, dtype=jnp.int32)[None, :]).astype(
        jnp.int32
    )
    before = jnp.cumsum(onehot, axis=0) - onehot
    places = (before[:, :, None] == jnp.arange(capacity, dtype=jnp.int32)[None, None, :]).astype(
        jnp.int32
    )
    chosen = onehot[:, :, None] * places
    return jnp.sum(chosen.reshape(tokens, -1, experts_count * capacity), axis=1)


def shards(
    inner_x,
    inner_z,
    step_raw,
    conv_weight,
    state_proj,
    step_bias,
    decay_log,
    skip_gain,
    moe_tokens,
    routes,
    gate_weight,
    up_weight,
):
    length = inner_x.shape[0]
    taps = conv_weight.shape[0]
    states = decay_log.shape[0]
    rim_rows = from_behind(inner_x[length - (taps - 1) :], "seq", 1)
    padded = jnp.concatenate([rim_rows, inner_x], axis=0).astype(jnp.float32)
    conv_sum = jnp.zeros(inner_x.shape, jnp.float32)
    for offset in range(taps):
        conv_sum = conv_sum + conv_weight[offset][None, :] * padded[offset : offset + length]
    conv_out = jax.nn.silu(conv_sum)
    partial_coef = jnp.dot(
        conv_out.astype(jnp.bfloat16), state_proj, preferred_element_type=jnp.float32
    )
    coeffs = lax.psum(partial_coef, "exp")
    input_coef = coeffs[:, :states]
    output_coef = coeffs[:, states:]
    step_size = jax.nn.softplus(step_raw.astype(jnp.float32) + step_bias[None, :])
    rates = -jnp.exp(decay_log)
    cumulative = jnp.cumsum(step_size, axis=0)
    total_step = cumulative[-1]
    end_decay = jnp.exp(rates * total_step[None, :])
    remaining = total_step[None, :] - cumulative
    weighted_input = step_size * conv_out
    end_state = jnp.sum(
        jnp.exp(rates[None, :, :] * remaining[:, None, :])
        * input_coef[:, :, None]
        * weighted_input[:, None, :],
        axis=0,
    )
    flight = lax.axis_size("exp")
    table = slot_table(routes.reshape(-1), flight, CAP, routes.shape[0])
    placed = jnp.dot(
        table.T.astype(jnp.bfloat16), moe_tokens, preferred_element_type=jnp.float32
    ).astype(jnp.bfloat16)
    placed = placed.reshape(flight, CAP, moe_tokens.shape[1])
    identity = (jnp.ones(end_decay.shape, jnp.float32), jnp.zeros(end_state.shape, jnp.float32))
    _, incoming = carried_in((end_decay, end_state), "seq", pair_combine, identity)

    def advance(state, row):
        step_row, in_row, out_row, drive_row = row
        state = jnp.exp(rates * step_row[None, :]) * state + in_row[:, None] * drive_row[None, :]
        return (state, jnp.sum(out_row[:, None] * state, axis=0))

    _, scan_out = lax.scan(
        advance, incoming, (step_size, input_coef, output_coef, weighted_input), unroll=8
    )
    result = (scan_out + skip_gain[None, :] * conv_out) * jax.nn.silu(inner_z.astype(jnp.float32))
    mixed = result.astype(jnp.bfloat16)
    arrived = lax.all_to_all(placed, "exp", split_axis=0, concat_axis=2, tiled=True)
    hidden = expand_rows(
        lax.all_gather(arrived[0], "seq", axis=0, tiled=True), gate_weight[0], up_weight[0]
    )[None]
    return (mixed, hidden)


def solution(mesh):
    return jax.shard_map(
        shards,
        mesh=mesh,
        in_specs=(
            P("seq", "exp"),
            P("seq", "exp"),
            P("seq", "exp"),
            P(None, "exp"),
            P("exp", None),
            P("exp"),
            P(None, "exp"),
            P("exp"),
            P("seq", "exp"),
            P("seq", None),
            P("exp", "seq", None),
            P("exp", "seq", None),
        ),
        out_specs=(P("seq", "exp"), P("exp", "seq", None)),
        check_vma=False,
    )
```

profile of v0, /device:TPU:0, one launch (start us, length us, event | category | flops | bytes accessed | tf_op | source)
XLA Modules:
  0.0 276.9 jit_solution(13105242595700534177)
XLA Ops:
  8.1 2.4 collective-permute-start
  15.5 3.6 %all-to-all-start = ((bf16[2,20,2048]{2,1,0:T(8,128)(2,1)}), bf16[2,20,2048]{2,1,0:T(8,128)(2,1)S(1)}, u32[]{:S(2)}, u32[]{:S(2)}) async-start(bf16[2,20,2048]{2,1,0:T(8,128)(2,1)} %reshape.175), calls=%async_computation | async-start | bytes 393216 | tf_op jit(solution)/shard_map/all_to_all | solution.py:113
  20.7 3.4 %all-to-all-done = bf16[2,20,2048]{2,1,0:T(8,128)(2,1)S(1)} async-done(((bf16[2,20,2048]{2,1,0:T(8,128)(2,1)}), bf16[2,20,2048]{2,1,0:T(8,128)(2,1)S(1)}, u32[]{:S(2)}, u32[]{:S(2)}) %all-to-all-start) | async-done | bytes 163872 | tf_op jit(solution)/shard_map/all_to_all | solution.py:113
  25.1 5.3 %fusion.34 = (f32[128,4096]{1,0:T(8,128)}, f32[128,4096]{1,0:T(8,128)}, f32[16,8,4096]{2,1,0:T(8,128)}, f32[128,4096]{1,0:T(8,128)}) fusion(f32[4096]{0:T(1024)S(1)} %copy-done.7, bf16[128,4096]{1,0:T(8,128)(2,1)} %param.18, f32[131,4096]{1,0:T(8,128)S(1)} %maximum_convert_fusion, f32[4096]{0:T(1024)S(1)} %bitcast.234, f32[4096]{0:T(1024)S(1)} %bitcast.235, ...), kind=kLoop, calls=%fused_computation.98 | loop fusion | flops 10485760 | bytes 17907712 | tf_op jit(solution)/shard_map/mul | solution.py:87
  30.4 4.8 %reduce_window_sum.26 = f32[128,4096]{1,0:T(8,128)} reduce-window(f32[128,4096]{1,0:T(8,128)} %get-tuple-element.247, f32[]{:T(128)} %constant.60.clone.1), window={size=128x1 pad=127_0x0_0}, to_apply=%region_0.1 | reduce-window | flops 66584576 | bytes 4194308 | tf_op jit(solution)/shard_map/jit(cumsum)/reduce_window_sum | solution.py:83
  36.6 6.7 %psum.7 = f32[128,32]{0,1:T(8,128)S(1)} all-reduce(f32[128,32]{0,1:T(8,128)S(1)} %fusion.28), channel_id=1, replica_groups=mesh['seq'=16,'exp'=2] {'exp'}, use_global_device_ids=true, to_apply=%region_1.2 | all-reduce | flops 4096 | bytes 32768 | tf_op jit(solution)/shard_map/psum | solution.py:78
  46.5 7.7 %multiply_reduce_fusion.8 = f32[16,4096]{1,0:T(8,128)} fusion(f32[128,4096]{1,0:T(8,128)S(1)} %copy-done.2, f32[128,16]{1,0:T(8,128)S(1)} %copy.35, f32[128,4096]{1,0:T(8,128)S(1)} %broadcast_subtract_fusion, f32[16,4096]{1,0:T(8,128)S(1)} %get-tuple-element.449), kind=kLoop, calls=%fused_computation.54 | loop fusion | flops 33488896 | bytes 4726784 | tf_op jit(solution)/shard_map/reduce_sum | solution.py:88
  55.1 16.3 %all-gather.11.cloned.1.call-done = bf16[16,20,4096]{2,1,0:T(8,128)(2,1)} async-done(((bf16[1,20,4096]{2,1,0:T(8,128)(2,1)}), bf16[16,20,4096]{2,1,0:T(8,128)(2,1)}) %all-gather.11.cloned.1.call-update) | async-done | bytes 2621456 | tf_op jit(solution)/shard_map/all_gather | solution.py:115
  71.3 4.2 %reshape.179 = bf16[320,4096]{1,0:T(8,128)(2,1)} reshape(bf16[16,20,4096]{2,1,0:T(8,128)(2,1)} %all-gather.11.cloned.1.call-done) | data formatting | bytes 5242880
  75.6 5.9 %fusion.13 = f32[768,320]{0,1:T(8,128)S(1)} fusion(bf16[320,4096]{1,0:T(8,128)(2,1)} %reshape.179, bf16[1,768,4096]{2,1,0:T(8,128)(2,1)} %param.26), kind=kOutput, calls=%fused_computation.77 | convolution fusion | flops 2013265920 | bytes 9895936 | tf_op jit(solution)/shard_map/dot_general | solution.py:35
  81.6 5.9 %fusion.25 = bf16[1,768,320]{1,2,0:T(8,128)(2,1)} fusion(bf16[320,4096]{1,0:T(8,128)(2,1)S(1)} %copy-done.3, bf16[1,768,4096]{2,1,0:T(8,128)(2,1)} %param.27, f32[768,320]{0,1:T(8,128)S(1)} %fusion.13), kind=kOutput, calls=%fused_computation.81 | convolution fusion | flops 2014740480 | bytes 10387456 | tf_op jit(solution)/shard_map/dot_general | solution.py:36
  87.4 35.6 %all-gather.9.cloned.1.call-done = f32[256,4096]{1,0:T(8,128)} async-done(((f32[16,4096]{1,0:T(8,128)}), f32[256,4096]{1,0:T(8,128)}) %all-gather.9.cloned.1.call-update) | async-done | bytes 4194320 | tf_op jit(solution)/shard_map/all_gather | solution.py:17
  123.1 51.8 %all-gather.7.cloned.1.call-done = f32[256,4096]{1,0:T(8,128)} async-done(((f32[16,4096]{1,0:T(8,128)}), f32[256,4096]{1,0:T(8,128)}) %all-gather.7.cloned.1.call-update) | async-done | bytes 4194320 | tf_op jit(solution)/shard_map/all_gather | solution.py:17
  174.9 19.1 %while.27 = (s32[]{:T(128)}, f32[16,4096]{1,0:T(8,128)S(1)}, s32[]{:T(128)}, f32[16,16,4096]{2,1,0:T(8,128)}, f32[16,16,4096]{2,1,0:T(8,128)}, /*index=5*/s32[]{:T(128)}, s32[]{:T(128)}) while((s32[]{:T(128)}, f32[16,4096]{1,0:T(8,128)S(1)}, s32[]{:T(128)}, f32[16,16,4096]{2,1,0:T(8,128)}, f32[16,16,4096]{2,1,0:T(8,128)}, ...), condition=%wide.region_4.5_spmd.clone, body=%wide.region_3.4_spmd.clone.sunk | while | flops 262148 | bytes 1048677 | solution.py:26
  194.0 72.8 %while.26 = (s32[]{:T(128)}, f32[16,4096]{1,0:T(8,128)S(1)}, f32[16,8,4096]{2,1,0:T(8,128)}, f32[16,8,4096]{2,1,0:T(8,128)}, f32[16,4096]{1,0:T(8,128)S(1)}, /*i...) while((s32[]{:T(128)}, f32[16,4096]{1,0:T(8,128)S(1)}, ...), condition=%wide.region_14.15_spmd, body=%wide.region_5.14_spmd.sunk | while | flops 4685833 | bytes 3741845 | solution.py:108
  194.0 2.4 constant_dynamic-slice_fusion.21
  207.4 2.4 constant_dynamic-slice_fusion.21
  220.9 2.7 constant_dynamic-slice_fusion.21
  225.7 2.7 constant_dynamic-slice_fusion.21
  235.0 2.4 constant_dynamic-slice_fusion.21
  244.1 2.4 constant_dynamic-slice_fusion.21
  253.1 2.4 constant_dynamic-slice_fusion.21
  262.1 2.5 constant_dynamic-slice_fusion.21
  266.8 3.6 %fusion.12 = bf16[128,4096]{1,0:T(8,128)(2,1)} fusion(bf16[128,4096]{1,0:T(8,128)(2,1)} %param.17, f32[128,4096]{1,0:T(8,128)S(1)} %copy-done.1, f32[16,8,4096]{2,1,0:T(8,128)} %get-tuple-element.139, f32[4096]{0:T(1024)S(1)} %copy-done.8), kind=kLoop, calls=%fused_computation.76 | loop fusion | flops 4718592 | bytes 6307840 | tf_op jit(solution)/shard_map/convert_element_type | solution.py:112
  (211 shorter events, 84.6 us)
Async XLA Ops:
  7.2 7.3 %copy-start = (bf16[128,2048]{1,0:T(8,128)(2,1)S(1)}, bf16[128,2048]{1,0:T(8,128)(2,1)}, u32[]{:S(2)}) copy-start(bf16[128,2048]{1,0:T(8,128)(2,1)} %param.24) | copy-start | bytes 1572868
  7.2 11.9 %copy-start.6 = (f32[4,4096]{1,0:T(4,128)S(1)}, f32[4,4096]{1,0:T(4,128)}, u32[]{:S(2)}) copy-start(f32[4,4096]{1,0:T(4,128)} %param.19) | copy-start | bytes 196612
  8.1 11.0 %collective-permute-start = (bf16[3,4096]{1,0:T(4,128)(2,1)S(1)}, bf16[3,4096]{1,0:T(4,128)(2,1)S(1)}, u32[]{:S(2)}, u32[]{:S(2)}) collective-permute-start(bf16[3,4096]{1,0:T(4,128)(2,1)S(1)} %slice.172), channel_id=1, source_target_pairs={{0,2},{2,4},{4,6},{6,8},{8,10},{10,12},{12,14},{14,16},{16,18},{18... | collective-permute-start | bytes 73736 | tf_op jit(solution)/shard_map/ppermute | solution.py:12
  15.5 8.6 %all-to-all-start = ((bf16[2,20,2048]{2,1,0:T(8,128)(2,1)}), bf16[2,20,2048]{2,1,0:T(8,128)(2,1)S(1)}, u32[]{:S(2)}, u32[]{:S(2)}) async-start(bf16[2,20,2048]{2,1,0:T(8,128)(2,1)} %reshape.175), calls=%async_computation | async-start | bytes 393216 | tf_op jit(solution)/shard_map/all_to_all | solution.py:113
  19.1 52.3 %all-gather.11.cloned.1.call-start = ((), (), s32[]{:S(2)}) async-start(), calls=%async_computation.3 | async-start | bytes 3342336 | tf_op jit(solution)/shard_map/all_gather | solution.py:115
  19.1 5.9 %copy-start.7 = (f32[4096]{0:T(1024)S(1)}, f32[4096]{0:T(1024)}, u32[]{:S(2)}) copy-start(f32[4096]{0:T(1024)} %param.21) | copy-start | bytes 49156
  25.0 98.0 %all-gather.9.cloned.1.call-start = ((), (), s32[]{:S(2)}) async-start(), calls=%async_computation.2 | async-start | bytes 4456448 | tf_op jit(solution)/shard_map/all_gather | solution.py:17
  30.4 5.7 %copy-start.1 = (f32[128,4096]{1,0:T(8,128)S(1)}, f32[128,4096]{1,0:T(8,128)}, u32[]{:S(2)}) copy-start(f32[128,4096]{1,0:T(8,128)} %get-tuple-element.203) | copy-start | bytes 6291460
  30.4 5.8 %copy-start.4 = (bf16[4096,32]{0,1:T(8,128)(2,1)S(1)}, bf16[4096,32]{0,1:T(8,128)(2,1)}, u32[]{:S(2)}) copy-start(bf16[4096,32]{0,1:T(8,128)(2,1)} %param.20) | copy-start | bytes 786436
  35.2 8.3 %copy-start.5 = (f32[16,4096]{1,0:T(8,128)S(1)}, f32[16,4096]{1,0:T(8,128)}, u32[]{:S(2)}) copy-start(f32[16,4096]{1,0:T(8,128)} %param.22) | copy-start | bytes 786436
  44.3 2.2 copy-start.2
  54.2 120.7 %all-gather.7.cloned.1.call-start = ((), (), s32[]{:S(2)}) async-start(), calls=%async_computation.1 | async-start | bytes 4456448 | tf_op jit(solution)/shard_map/all_gather | solution.py:17
  75.6 6.0 %copy-start.3 = (bf16[320,4096]{1,0:T(8,128)(2,1)S(1)}, bf16[320,4096]{1,0:T(8,128)(2,1)}, u32[]{:S(2)}) copy-start(bf16[320,4096]{1,0:T(8,128)(2,1)} %reshape.179) | copy-start | bytes 7864324
  194.0 72.9 %copy-start.8 = (f32[4096]{0:T(1024)S(1)}, f32[4096]{0:T(1024)}, u32[]{:S(2)}) copy-start(f32[4096]{0:T(1024)} %param.23) | copy-start | bytes 49156
Sparse Core Ops, SparseCore 0:
  25.1 46.1 all-gather.10
  73.5 49.5 all-gather.8
  125.8 49.0 all-gather.6
where the time goes:
time: 278 us; the launch traced here: 277 us
  waiting for transfers between devices  108 us (39%)
  other arithmetic  64.9 us (23%)
  local copies, waits for them, and re-layouts  63.6 us (23%)
  between operations  14 us (5%)
  matrix products  12.5 us (4%)
  blocking collectives  6.73 us (2%)
  starting transfers between devices  6.24 us (2%)
    all_gather x2, waiting for transfers between devices, carried_in(): pieces = jax.tree.map(lambda part: lax.all_gather(part, axis), value)  87.5 us
    slice x16, local copies, waits for them, and re-layouts, shards(): lax.scan(advance, incoming, (step_size, input_coef, output_coef, weighted...  38.2 us
    reduce_sum x48, other arithmetic, advance(): return (state, jnp.sum(out_row[:, None] * state, axis=0))  19.5 us
    select_n x15, other arithmetic, turn(): jnp.where(position < mine, new, old)  18.7 us
    all_gather x1, waiting for transfers between devices, shards(): lax.all_gather(arrived[0], 'seq', axis=0, tiled=True)  16.3 us
    dynamic_update_slice x16, local copies, waits for them, and re-layouts, shards(): lax.scan(advance, incoming, (step_size, input_coef, output_coef, weighted...  10.6 us
    reduce_sum x1, other arithmetic, shards(): jnp.sum(jnp.exp(rates[None, :, :] * remaining[:, None, :]) * input_coef[:...  7.69 us
    psum x1, blocking collectives, shards(): coeffs = lax.psum(partial_coef, 'exp')  6.73 us
  transfers between devices with their start and end apart: 5, of which 4 were waited for; matrix products, arithmetic and copies ran while one was open for 16% of the time, Pallas kernels for 0%

commit v1 on v0

v1 whole, which is shorter than its diff:
```python
import functools

import jax
import jax.numpy as jnp
from jax import lax
from jax.experimental import pallas as pl
from jax.experimental.pallas import tpu as pltpu
from jax.sharding import PartitionSpec as P

CAP = 20
LANES = 128
SUB = 8
LOG2E = 1.4426950408889634
MESH = pl.DeviceIdType.MESH
VMEM_LIMIT = 48 * 1024 * 1024


def silu(value):
    half = 0.5 * value
    return half + half * jnp.tanh(half)


def softplus(value):
    grown = jnp.exp(value)
    series = grown * (1.0 - grown * (0.5 - grown * (1.0 / 3.0 - 0.25 * grown)))
    return jnp.where(grown < 0.03, series, jnp.log(1.0 + grown))


def front_kernel(
    x_ref, rim_ref, raw_ref, taps_ref, proj_ref, bias_ref, conv_ref, step_ref, drive_ref, coef_ref, wide, rounded
):
    length, channels = x_ref.shape
    taps = taps_ref.shape[0]

    def tile(position, carry):
        lanes = pl.ds(pl.multiple_of(position * LANES, LANES), LANES)
        rows = pl.ds(pl.multiple_of(position * length, length), length)
        wide[pl.ds(0, 16), :] = rim_ref[:, lanes].astype(jnp.float32)
        wide[pl.ds(16, length), :] = x_ref[:, lanes].astype(jnp.float32)
        total = taps_ref[pl.ds(0, 1), lanes] * wide[pl.ds(17 - taps, length), :]
        for tap in range(1, taps):
            total = total + taps_ref[pl.ds(tap, 1), lanes] * wide[pl.ds(17 - taps + tap, length), :]
        conv = silu(total)
        step = softplus(raw_ref[:, lanes].astype(jnp.float32) + bias_ref[:, lanes])
        conv_ref[rows, :] = conv
        step_ref[rows, :] = step
        drive_ref[rows, :] = step * conv
        rounded[:, lanes] = conv.astype(jnp.bfloat16)
        return carry

    lax.fori_loop(0, channels // LANES, tile, 0)
    coef_ref[...] = jnp.dot(rounded[...], proj_ref[...], preferred_element_type=jnp.float32)


def splat_columns(coef_ref, first, count, table):
    length = coef_ref.shape[0]
    for column in range(count):
        table[pl.ds(column * length, length), :] = jnp.broadcast_to(
            coef_ref[:, first + column : first + column + 1], (length, LANES)
        )


def rate_rows(decay_ref, table):
    states, channels = decay_ref.shape

    def tile(position, carry):
        lanes = pl.ds(pl.multiple_of(position * LANES, LANES), LANES)
        rows = pl.ds(pl.multiple_of(position * states, states), states)
        table[rows, :] = jnp.exp(decay_ref[:, lanes]) * (-LOG2E)
        return carry

    lax.fori_loop(0, channels // LANES, tile, 0)


def first_kernel(step_ref, drive_ref, coef_ref, decay_ref, end_ref, total_ref, rate_ref, in_table):
    states, channels = decay_ref.shape
    length = coef_ref.shape[0]
    groups = channels // (LANES * SUB)
    splat_columns(coef_ref, 0, states, in_table)
    rate_rows(decay_ref, rate_ref)

    def group(position, carry):
        base = position * SUB
        rates = [rate_ref[pl.ds(base * states + n, SUB, stride=states), :] for n in range(states)]

        def block(turn, held):
            total, state = held[0], list(held[1:])
            for inner in range(4):
                t = turn * 4 + inner
                step = step_ref[pl.ds(base * length + t, SUB, stride=length), :]
                drive = drive_ref[pl.ds(base * length + t, SUB, stride=length), :]
                total = total + step
                for n in range(states):
                    row = in_table[pl.ds(n * length + t, 1), :]
                    state[n] = jnp.exp2(rates[n] * step) * state[n] + row * drive
            return (total, *state)

        zero = jnp.zeros((SUB, LANES), jnp.float32)
        held = lax.fori_loop(0, length // 4, block, (zero,) * (states + 1))
        total_ref[pl.ds(pl.multiple_of(base, SUB), SUB), :] = held[0]
        for n in range(states):
            end_ref[pl.ds(base * states + n, SUB, stride=states), :] = held[1 + n]
        return carry

    lax.fori_loop(0, groups, group, 0)


def second_kernel(
    step_ref, drive_ref, conv_ref, z_ref, coef_ref, rate_ref, start_ref, gain_ref, mixed_ref, in_table, out_table, sums
):
    length, channels = z_ref.shape
    states = coef_ref.shape[1] // 2
    groups = channels // (LANES * SUB)
    splat_columns(coef_ref, 0, states, in_table)
    splat_columns(coef_ref, states, states, out_table)

    def group(position, carry):
        base = position * SUB
        rates = [rate_ref[pl.ds(base * states + n, SUB, stride=states), :] for n in range(states)]
        start = tuple(
            start_ref[pl.ds(base * states + n, SUB, stride=states), :] for n in range(states)
        )

        def block(turn, held):
            state = list(held)
            for inner in range(4):
                t = turn * 4 + inner
                step = step_ref[pl.ds(base * length + t, SUB, stride=length), :]
                drive = drive_ref[pl.ds(base * length + t, SUB, stride=length), :]
                parts = [None, None]
                for n in range(states):
                    row = in_table[pl.ds(n * length + t, 1), :]
                    state[n] = jnp.exp2(rates[n] * step) * state[n] + row * drive
                    term = out_table[pl.ds(n * length + t, 1), :] * state[n]
                    parts[n % 2] = term if parts[n % 2] is None else parts[n % 2] + term
                sums[pl.ds(base * length + t, SUB, stride=length), :] = parts[0] + parts[1]
            return tuple(state)

        lax.fori_loop(0, length // 4, block, start)
        return carry

    lax.fori_loop(0, groups, group, 0)

    def tile(position, carry):
        lanes = pl.ds(pl.multiple_of(position * LANES, LANES), LANES)
        rows = pl.ds(pl.multiple_of(position * length, length), length)
        result = sums[rows, :] + gain_ref[:, lanes] * conv_ref[rows, :]
        mixed_ref[:, lanes] = (result * silu(z_ref[:, lanes].astype(jnp.float32))).astype(jnp.bfloat16)
        return carry

    lax.fori_loop(0, channels // LANES, tile, 0)


def carry_kernel(
    count, end_ref, total_ref, rate_ref, start_ref, got_end, got_total, leaving, sends, arrivals
):
    me, side = lax.axis_index("seq"), lax.axis_index("exp")
    piece = end_ref.shape[1]

    def peer_of(distance):
        return lax.rem(me + distance, count)

    barrier = pltpu.get_barrier_semaphore()

    def greet(distance, carry):
        pl.semaphore_signal(barrier, inc=1, device_id=(peer_of(distance), side), device_id_type=MESH)
        return carry

    lax.fori_loop(1, count, greet, 0)
    pl.semaphore_wait(barrier, count - 1)

    def end_copy(distance):
        peer = peer_of(distance)
        return pltpu.make_async_remote_copy(
            end_ref.at[peer], got_end.at[me], sends.at[0, distance], arrivals.at[0, distance],
            device_id=(peer, side), device_id_type=MESH,
        )

    def total_copy(distance):
        peer = peer_of(distance)
        return pltpu.make_async_remote_copy(
            total_ref.at[peer], got_total.at[me], sends.at[1, distance], arrivals.at[1, distance],
            device_id=(peer, side), device_id_type=MESH,
        )

    def back_copy(distance):
        peer = peer_of(distance)
        return pltpu.make_async_remote_copy(
            leaving.at[peer], start_ref.at[me], sends.at[2, distance], arrivals.at[2, distance],
            device_id=(peer, side), device_id_type=MESH,
        )

    def send(distance, carry):
        end_copy(distance).start()
        total_copy(distance).start()
        return carry

    lax.fori_loop(1, count, send, 0)
    got_end[me] = end_ref[me]
    got_total[me] = total_ref[me]

    def receive(distance, carry):
        end_copy(distance).wait()
        total_copy(distance).wait()
        return carry

    lax.fori_loop(1, count, receive, 0)
    rates = rate_ref[me]
    spread = got_total.shape[1]

    def join(source, state):
        leaving[source] = state.astype(jnp.bfloat16)
        totals = got_total[source]
        totals = jnp.broadcast_to(totals[:, None, :], (spread, piece // spread, LANES)).reshape(piece, LANES)
        return jnp.exp2(rates * totals) * state + got_end[source].astype(jnp.float32)

    lax.fori_loop(0, count, join, jnp.zeros((piece, LANES), jnp.float32))

    def send_back(distance, carry):
        back_copy(distance).start()
        return carry

    lax.fori_loop(1, count, send_back, 0)
    start_ref[me] = leaving[me]

    def receive_back(distance, carry):
        back_copy(distance).wait()
        return carry

    lax.fori_loop(1, count, receive_back, 0)


def expand_rows(slot_rows, gate_matrix, up_matrix):
    dims = (((1,), (1,)), ((), ()))
    gate_part = lax.dot_general(gate_matrix, slot_rows, dims, preferred_element_type=jnp.float32)
    up_part = lax.dot_general(up_matrix, slot_rows, dims, preferred_element_type=jnp.float32)
    return (jax.nn.silu(gate_part) * up_part).astype(jnp.bfloat16)


def slot_table(pair_ids, experts_count, capacity, tokens):
    onehot = (pair_ids[:, None] == jnp.arange(experts_count, dtype=jnp.int32)[None, :]).astype(
        jnp.int32
    )
    before = jnp.cumsum(onehot, axis=0) - onehot
    places = (before[:, :, None] == jnp.arange(capacity, dtype=jnp.int32)[None, None, :]).astype(
        jnp.int32
    )
    chosen = onehot[:, :, None] * places
    return jnp.sum(chosen.reshape(tokens, -1, experts_count * capacity), axis=1)


def f32(*shape):
    return jax.ShapeDtypeStruct(shape, jnp.float32)


def kernel_call(body, outs, scratch, **params):
    return pl.pallas_call(
        body,
        out_shape=outs,
        scratch_shapes=scratch,
        compiler_params=pltpu.CompilerParams(vmem_limit_bytes=VMEM_LIMIT, **params),
    )


def shards(
    inner_x,
    inner_z,
    step_raw,
    conv_weight,
    state_proj,
    step_bias,
    decay_log,
    skip_gain,
    moe_tokens,
    routes,
    gate_weight,
    up_weight,
):
    length, channels = inner_x.shape
    states = decay_log.shape[0]
    count, flight = lax.axis_size("seq"), lax.axis_size("exp")
    rim = lax.ppermute(inner_x[length - 16 :], "seq", [(s, s + 1) for s in range(count - 1)])
    table = slot_table(routes.reshape(-1), flight, CAP, routes.shape[0])
    placed = jnp.dot(
        table.T.astype(jnp.bfloat16), moe_tokens, preferred_element_type=jnp.float32
    ).astype(jnp.bfloat16)
    placed = placed.reshape(flight, CAP, moe_tokens.shape[1])
    arrived = lax.all_to_all(placed, "exp", split_axis=0, concat_axis=2, tiled=True)
    slot_rows = lax.all_gather(arrived[0], "seq", axis=0, tiled=True)

    tiles = channels // LANES
    flat = f32(tiles * length, LANES)
    conv, step, drive, partial_coef = kernel_call(
        front_kernel,
        (flat, flat, flat, f32(length, 2 * states)),
        [pltpu.VMEM((length + 16, LANES), jnp.float32), pltpu.VMEM((length, channels), jnp.bfloat16)],
    )(inner_x, rim, step_raw, conv_weight, state_proj, step_bias[None, :])
    coeffs = lax.psum(partial_coef, "exp")
    wide_table = pltpu.VMEM((states * length, LANES), jnp.float32)
    end, total, rates = kernel_call(
        first_kernel,
        (f32(tiles * states, LANES), f32(tiles, LANES), f32(tiles * states, LANES)),
        [wide_table],
    )(step, drive, coeffs, decay_log)
    piece = tiles * states // count
    spread = max(1, piece // states)
    share = max(1, states // piece)
    totals = jnp.broadcast_to(
        total.reshape(tiles // spread, 1, spread, LANES), (tiles // spread, share, spread, LANES)
    ).reshape(count, spread, LANES)
    pieces = (count, piece, LANES)
    start = kernel_call(
        functools.partial(carry_kernel, count),
        jax.ShapeDtypeStruct(pieces, jnp.bfloat16),
        [
            pltpu.VMEM(pieces, jnp.bfloat16),
            pltpu.VMEM(totals.shape, jnp.float32),
            pltpu.VMEM(pieces, jnp.bfloat16),
            pltpu.SemaphoreType.DMA((3, count)),
            pltpu.SemaphoreType.DMA((3, count)),
        ],
        collective_id=0,
        has_side_effects=True,
    )(end.astype(jnp.bfloat16).reshape(pieces), totals, rates.reshape(pieces))
    mixed = kernel_call(
        second_kernel,
        jax.ShapeDtypeStruct((length, channels), jnp.bfloat16),
        [wide_table, wide_table, pltpu.VMEM((tiles * length, LANES), jnp.float32)],
    )(
        step, drive, conv, inner_z, coeffs, rates,
        start.astype(jnp.float32).reshape(tiles * states, LANES), skip_gain[None, :],
    )
    hidden = expand_rows(slot_rows, gate_weight[0], up_weight[0])[None]
    return (mixed, hidden)


def solution(mesh):
    return jax.shard_map(
        shards,
        mesh=mesh,
        in_specs=(
            P("seq", "exp"),
            P("seq", "exp"),
            P("seq", "exp"),
            P(None, "exp"),
            P("exp", None),
            P("exp"),
            P(None, "exp"),
            P("exp"),
            P("seq", "exp"),
            P("seq", None),
            P("exp", "seq", None),
            P("exp", "seq", None),
        ),
        out_specs=(P("seq", "exp"), P("exp", "seq", None)),
        check_vma=False,
    )
```

time: 278 us -> 113 us (0.41)
  waiting for transfers between devices: 108 us -> 0.49 us
  other arithmetic: 64.9 us -> 1.15 us
  Pallas kernels: 0 us -> 52.4 us
  local copies, waits for them, and re-layouts: 63.6 us -> 14.6 us
  blocking collectives: 6.73 us -> 16.3 us
  starting transfers between devices: 6.24 us -> 1.47 us
    all_gather x3 -> x1, waiting for transfers between devices: 104 us -> 0.01 us  [shards(): slot_rows = lax.all_gather(arrived[0], 'seq', axis=0, tiled=True)]
    pallas_call x0 -> x4, Pallas kernels: none -> 52.4 us  [the longest x1 22.4 us: shards(): kernel_call(functools.partial(carry_kernel, count), jax.ShapeDtypeStruct(...]
    slice x23 -> x2, local copies, waits for them, and re-layouts: 40.6 us -> 0.22 us  [the longest x16 38.2 us: shards(): lax.scan(advance, incoming, (step_size, input_coef, output_coef, weighted...]
    reduce_sum x49 -> x0, other arithmetic: 27.2 us -> none  [the longest x48 19.5 us: advance(): return (state, jnp.sum(out_row[:, None] * state, axis=0))]
    select_n x15 -> x0, other arithmetic: 18.7 us -> none  [turn(): jnp.where(position < mine, new, old)]
    dynamic_update_slice x16 -> x0, local copies, waits for them, and re-layouts: 10.6 us -> none  [shards(): lax.scan(advance, incoming, (step_size, input_coef, output_coef, weighted...]
    all_to_all x0 -> x1, blocking collectives: none -> 8.86 us  [shards(): lax.all_to_all(placed, 'exp', split_axis=0, concat_axis=2, tiled=True)]
    unnamed x21 -> x32, local copies, waits for them, and re-layouts: 6.12 us -> 12.3 us
  transfers between devices with their start and end apart: 5 -> 2, of which waited for: 4 -> 1; matrix products, arithmetic and copies ran while one was open for 16% -> 0% of each run, Pallas kernels for 0% -> 46%
where the time goes in v1:
time: 113 us
  Pallas kernels  52.4 us (46%)
  blocking collectives  16.3 us (14%)
  local copies, waits for them, and re-layouts  14.6 us (13%)
  between operations  14.3 us (13%)
  matrix products  12.1 us (11%)
  starting transfers between devices  1.47 us (1%)
  other arithmetic  1.15 us (1%)
    pallas_call x1, Pallas kernels, shards(): kernel_call(functools.partial(carry_kernel, count), jax.ShapeDtypeStruct(...  22.4 us
    pallas_call x1, Pallas kernels, shards(): kernel_call(second_kernel, jax.ShapeDtypeStruct((length, channels), jnp.b...  16.1 us
    unnamed x32, local copies, waits for them, and re-layouts  12.3 us
    pallas_call x1, Pallas kernels, shards(): kernel_call(first_kernel, (f32(tiles * states, LANES), f32(tiles, LANES),...  9.32 us
    all_to_all x1, blocking collectives, shards(): lax.all_to_all(placed, 'exp', split_axis=0, concat_axis=2, tiled=True)  8.86 us
    psum x1, blocking collectives, shards(): coeffs = lax.psum(partial_coef, 'exp')  7.46 us
    dot_general x1, matrix products, expand_rows(): lax.dot_general(gate_matrix, slot_rows, dims, preferred_element_type=jnp....  5.95 us
    dot_general x1, matrix products, expand_rows(): lax.dot_general(up_matrix, slot_rows, dims, preferred_element_type=jnp.fl...  5.86 us
  transfers between devices with their start and end apart: 2, of which 1 were waited for; matrix products, arithmetic and copies ran while one was open for 0% of the time, Pallas kernels for 46%

profile of v1, /device:TPU:0, one launch (start us, length us, event | category | flops | bytes accessed | tf_op | source)
XLA Modules:
  0.0 112.7 jit_solution(10115561151775575981)
XLA Ops:
  7.2 0.9 copy.24
  8.4 0.6 reduce-window.6
  9.7 0.3 eq.57
  10.0 0.3 eq.58
  10.5 0.3 mul.17
  10.8 0.3 mul.18
  11.4 0.2 convolution_convert_fusion
  11.7 8.9 %all_to_all.15 = bf16[2,20,2048]{2,1,0:T(8,128)(2,1)S(1)} all-to-all(bf16[2,20,2048]{2,1,0:T(8,128)(2,1)S(1)} %reshape.70), channel_id=1, replica_groups=mesh['seq'=16,'exp'=2] {'exp'}, dimensions={0} | all-to-all | bytes 327680 | tf_op jit(solution)/shard_map/all_to_all | solution.py:288
  20.7 0.8 reshape.73
  21.6 1.4 %collective-permute-start = (bf16[16,4096]{1,0:T(8,128)(2,1)S(1)}, bf16[16,4096]{1,0:T(8,128)(2,1)S(1)}, u32[]{:S(2)}, u32[]{:S(2)}) collective-permute-start(bf16[16,4096]{1,0:T(8,128)(2,1)S(1)} %slice.9), channel_id=1, source_target_pairs={{0,2},{2,4},{4,6},{6,8},{8,10},{10,12},{12,14},{14,16},{16,18},{18... | collective-permute-start | bytes 393224 | tf_op jit(solution)/shard_map/ppermute | solution.py:282
  23.0 0.5 copy.23.proj_ref
  23.5 0.5 collective-permute-done.rim_ref
  24.0 1.2 %copy-done.6 = bf16[128,4096]{1,0:T(8,128)(2,1)S(1)} copy-done((bf16[128,4096]{1,0:T(8,128)(2,1)S(1)}, bf16[128,4096]{1,0:T(8,128)(2,1)}, u32[]{:S(2)}) %copy-start.6) | copy-done | bytes 1048600
  25.2 4.6 %shard_map.131 = (f32[4096,128]{1,0:T(8,128)S(1)}, f32[4096,128]{1,0:T(8,128)}, f32[4096,128]{1,0:T(8,128)}, f32[128,32]{1,0:T(8,128)S(1)}) custom-call(bf16[128,4096]{1,0:T(8,128)(2,1)S(1)} %copy-done.5, bf16[16,4096]{1,0:T(8,128)(2,1)S(1)} %collective-permute-done.rim_ref, bf16[128,4096]{1,0:T(8,128)(2,1)S(1)} %copy-done.6, f32[4,4096]{1,0:T(4,128)S(1)} %copy-done.9, ...), custom_call_target="tpu_custom_call" | custom-call | tf_op jit(solution)/shard_map/pallas_call | solution.py:293
  29.8 1.4 %copy-done.4 = f32[4096,128]{1,0:T(8,128)} copy-done((f32[4096,128]{1,0:T(8,128)}, f32[4096,128]{1,0:T(8,128)S(1)}, u32[]{:S(2)}) %copy-start.4) | copy-done | bytes 2097176
  31.2 7.5 %psum.7.coef_ref = f32[128,32]{1,0:T(8,128)S(1)} all-reduce(f32[128,32]{1,0:T(8,128)S(1)} %get-tuple-element.12), channel_id=1, replica_groups=mesh['seq'=16,'exp'=2] {'exp'}, use_global_device_ids=true, to_apply=%region_0.0 | all-reduce | flops 4096 | bytes 32768 | tf_op jit(solution)/shard_map/psum | solution.py:298
  38.7 1.6 %copy-done.1 = f32[4096,128]{1,0:T(8,128)S(1)} copy-done((f32[4096,128]{1,0:T(8,128)S(1)}, f32[4096,128]{1,0:T(8,128)}, u32[]{:S(2)}) %copy-start.1) | copy-done | bytes 2097176
  40.3 1.6 %copy-done.3 = f32[4096,128]{1,0:T(8,128)S(1)} copy-done((f32[4096,128]{1,0:T(8,128)S(1)}, f32[4096,128]{1,0:T(8,128)}, u32[]{:S(2)}) %copy-start.3) | copy-done | bytes 2097176
  41.9 9.3 %shard_map.132 = (f32[512,128]{1,0:T(8,128)S(1)}, f32[32,128]{1,0:T(8,128)S(1)}, f32[512,128]{1,0:T(8,128)S(1)}) custom-call(f32[4096,128]{1,0:T(8,128)S(1)} %copy-done.1, f32[4096,128]{1,0:T(8,128)S(1)} %copy-done.3, f32[128,32]{1,0:T(8,128)S(1)} %psum.7.coef_ref, f32[16,4096]{1,0:T(8,128)S(1)} %copy-done.8), custom_call_target="tpu_custom_call" | custom-call | tf_op jit(solution)/shard_map/pallas_call | solution.py:300
  51.2 22.4 %shard_map.133 = bf16[16,32,128]{2,1,0:T(8,128)(2,1)S(1)} custom-call(bf16[16,32,128]{2,1,0:T(8,128)(2,1)S(1)} %bitcast.54, f32[16,2,128]{2,1,0:T(2,128)S(1)} %bitcast.57, f32[16,32,128]{2,1,0:T(8,128)S(1)} %bitcast.53), custom_call_target="tpu_custom_call" | custom-call | tf_op jit(solution)/shard_map/pallas_call | solution.py:312
  73.7 16.1 %shard_map.134 = bf16[128,4096]{1,0:T(8,128)(2,1)} custom-call(f32[4096,128]{1,0:T(8,128)S(1)} %copy-done.2, f32[4096,128]{1,0:T(8,128)S(1)} %copy-done.3, f32[4096,128]{1,0:T(8,128)} %copy-done.4, bf16[128,4096]{1,0:T(8,128)(2,1)S(1)} %copy-done.7, f32[128,32]{1,0:T(8,128)S(1)} %psum.7.coef_ref, f32[512,128]{1,0:T(8,128)S(1)} %get-tuple-element.13.rate_ref, ...), custom_call_target="tpu_custom_call" | custom-call | tf_op jit(solution)/shard_map/pallas_call | solution.py:325
  89.7 4.3 %reshape.74 = bf16[320,4096]{1,0:T(8,128)(2,1)} reshape(bf16[16,20,4096]{2,1,0:T(8,128)(2,1)} %all-gather.3.cloned.1.call-done) | data formatting | bytes 5242880
  94.0 6.0 %fusion.4 = f32[768,320]{0,1:T(8,128)S(1)} fusion(bf16[320,4096]{1,0:T(8,128)(2,1)} %reshape.74, bf16[1,768,4096]{2,1,0:T(8,128)(2,1)} %param.22), kind=kOutput, calls=%fused_computation.5 | convolution fusion | flops 2013265920 | bytes 9895936 | tf_op jit(solution)/shard_map/dot_general | solution.py:235
  100.0 5.9 %fusion.16 = bf16[1,768,320]{1,2,0:T(8,128)(2,1)} fusion(bf16[320,4096]{1,0:T(8,128)(2,1)S(1)} %copy-done.12, bf16[1,768,4096]{2,1,0:T(8,128)(2,1)} %param.23, f32[768,320]{0,1:T(8,128)S(1)} %fusion.4), kind=kOutput, calls=%fused_computation.9 | convolution fusion | flops 2014740480 | bytes 10387456 | tf_op jit(solution)/shard_map/dot_general | solution.py:236
  (45 shorter events, 1.7 us)
Async XLA Ops:
  7.2 4.2 %copy-start = (bf16[128,2048]{1,0:T(8,128)(2,1)S(1)}, bf16[128,2048]{1,0:T(8,128)(2,1)}, u32[]{:S(2)}) copy-start(bf16[128,2048]{1,0:T(8,128)(2,1)} %param.20) | copy-start | bytes 1572868
  7.2 14.4 %copy-start.5 = (bf16[128,4096]{1,0:T(8,128)(2,1)S(1)}, bf16[128,4096]{1,0:T(8,128)(2,1)}, u32[]{:S(2)}) copy-start(bf16[128,4096]{1,0:T(8,128)(2,1)} %x_ref.1) | copy-start | bytes 3145732
  7.2 15.8 %copy-start.13 = (bf16[4096,32]{0,1:T(8,128)(2,1)S(1)}, bf16[4096,32]{0,1:T(8,128)(2,1)}, u32[]{:S(2)}) copy-start(bf16[4096,32]{0,1:T(8,128)(2,1)} %param.16) | copy-start | bytes 786436
  7.2 82.5 %all-gather.3.cloned.1.call-start = ((), (), s32[]{:S(2)}) async-start(), calls=%async_computation.1 | async-start | bytes 3342336 | tf_op jit(solution)/shard_map/all_gather | solution.py:289
  10.3 13.7 %copy-start.9 = (f32[4,4096]{1,0:T(4,128)S(1)}, f32[4,4096]{1,0:T(4,128)}, u32[]{:S(2)}) copy-start(f32[4,4096]{1,0:T(4,128)} %taps_ref.1) | copy-start | bytes 196612
  10.3 13.6 %copy-start.10 = (f32[4096]{0:T(1024)S(1)}, f32[4096]{0:T(1024)}, u32[]{:S(2)}) copy-start(f32[4096]{0:T(1024)} %param.17) | copy-start | bytes 49156
  21.5 17.2 %copy-start.8 = (f32[16,4096]{1,0:T(8,128)S(1)}, f32[16,4096]{1,0:T(8,128)}, u32[]{:S(2)}) copy-start(f32[16,4096]{1,0:T(8,128)} %decay_ref.1) | copy-start | bytes 786436
  21.6 2.4 %collective-permute-start = (bf16[16,4096]{1,0:T(8,128)(2,1)S(1)}, bf16[16,4096]{1,0:T(8,128)(2,1)S(1)}, u32[]{:S(2)}, u32[]{:S(2)}) collective-permute-start(bf16[16,4096]{1,0:T(8,128)(2,1)S(1)} %slice.9), channel_id=1, source_target_pairs={{0,2},{2,4},{4,6},{6,8},{8,10},{10,12},{12,14},{14,16},{16,18},{18... | collective-permute-start | bytes 393224 | tf_op jit(solution)/shard_map/ppermute | solution.py:282
  24.0 1.2 %copy-start.6 = (bf16[128,4096]{1,0:T(8,128)(2,1)S(1)}, bf16[128,4096]{1,0:T(8,128)(2,1)}, u32[]{:S(2)}) copy-start(bf16[128,4096]{1,0:T(8,128)(2,1)} %raw_ref.1) | copy-start | bytes 3145732
  29.8 1.4 %copy-start.4 = (f32[4096,128]{1,0:T(8,128)}, f32[4096,128]{1,0:T(8,128)S(1)}, u32[]{:S(2)}) copy-start(f32[4096,128]{1,0:T(8,128)S(1)} %get-tuple-element.11.conv_ref) | copy-start | bytes 6291460
  38.7 1.6 %copy-start.1 = (f32[4096,128]{1,0:T(8,128)S(1)}, f32[4096,128]{1,0:T(8,128)}, u32[]{:S(2)}) copy-start(f32[4096,128]{1,0:T(8,128)} %get-tuple-element.9.step_ref) | copy-start | bytes 6291460
  40.3 1.6 %copy-start.3 = (f32[4096,128]{1,0:T(8,128)S(1)}, f32[4096,128]{1,0:T(8,128)}, u32[]{:S(2)}) copy-start(f32[4096,128]{1,0:T(8,128)} %get-tuple-element.10.drive_ref) | copy-start | bytes 6291460
  41.9 31.8 %copy-start.2 = (f32[4096,128]{1,0:T(8,128)S(1)}, f32[4096,128]{1,0:T(8,128)}, u32[]{:S(2)}) copy-start(f32[4096,128]{1,0:T(8,128)} %get-tuple-element.9.step_ref) | copy-start | bytes 6291460
  41.9 31.8 %copy-start.7 = (bf16[128,4096]{1,0:T(8,128)(2,1)S(1)}, bf16[128,4096]{1,0:T(8,128)(2,1)}, u32[]{:S(2)}) copy-start(bf16[128,4096]{1,0:T(8,128)(2,1)} %z_ref.1) | copy-start | bytes 3145732
  41.9 31.8 %copy-start.11 = (f32[4096]{0:T(1024)S(1)}, f32[4096]{0:T(1024)}, u32[]{:S(2)}) copy-start(f32[4096]{0:T(1024)} %param.19) | copy-start | bytes 49156
  94.0 6.0 %copy-start.12 = (bf16[320,4096]{1,0:T(8,128)(2,1)S(1)}, bf16[320,4096]{1,0:T(8,128)(2,1)}, u32[]{:S(2)}) copy-start(bf16[320,4096]{1,0:T(8,128)(2,1)} %reshape.74) | copy-start | bytes 7864324
Sparse Core Ops, SparseCore 0:
  21.7 49.2 all-gather.2

commit v2 on v0

v2 whole, which is shorter than its diff:
```python
import functools

import jax
import jax.numpy as jnp
from jax import lax
from jax.experimental import pallas as pl
from jax.experimental.pallas import tpu as pltpu
from jax.sharding import PartitionSpec as P

CAP = 20
LANES = 128
SUB = 8
LOG2E = 1.4426950408889634
MESH = pl.DeviceIdType.MESH
VMEM_LIMIT = 48 * 1024 * 1024


def silu(value):
    half = 0.5 * value
    return half + half * jnp.tanh(half)


def softplus(value):
    grown = jnp.exp(value)
    series = grown * (1.0 - grown * (0.5 - grown * (1.0 / 3.0 - 0.25 * grown)))
    return jnp.where(grown < 0.03, series, jnp.log(1.0 + grown))


def splat_columns(coef_ref, first, count, table):
    length = coef_ref.shape[0]
    for column in range(count):
        table[pl.ds(column * length, length), :] = jnp.broadcast_to(
            coef_ref[:, first + column : first + column + 1], (length, LANES)
        )


def rate_rows(decay_ref, table):
    states, channels = decay_ref.shape

    def tile(position, carry):
        lanes = pl.ds(pl.multiple_of(position * LANES, LANES), LANES)
        rows = pl.ds(pl.multiple_of(position * states, states), states)
        table[rows, :] = jnp.exp(decay_ref[:, lanes]) * (-LOG2E)
        return carry

    lax.fori_loop(0, channels // LANES, tile, 0)


def mixer_kernel(
    count, flight, x_ref, z_ref, raw_ref, taps_ref, proj_ref, bias_ref, decay_ref, gain_ref, tokens_ref, routes_ref,
    gate_hbm, up_hbm, mixed_ref, hidden_ref,
    gate_ref, up_ref, rim_ref, wide, rounded, conv_ref, step_ref, drive_ref, parts_ref, coef_ref, in_table, out_table,
    rate_ref, end_ref, total_ref, end_out, total_out, got_end, got_total, leaving, entering, start_ref, sums,
    stage, block_rows, rows_ref, order_ref,
    local_sem, rim_sem, pair_out, pair_in, rows_out, rows_in, sends, arrivals,
):
    length, channels = x_ref.shape
    states = decay_ref.shape[0]
    taps = taps_ref.shape[0]
    width = tokens_ref.shape[1]
    quarter = width // 4
    tiles = channels // LANES
    piece = tiles * states // count
    spread = got_total.shape[1]
    hidden_rows = gate_ref.shape[0]
    chunk = 256 if hidden_rows % 256 == 0 else hidden_rows
    me, side = lax.axis_index("seq"), lax.axis_index("exp")

    def seq_peer(distance):
        return lax.rem(me + distance, count)

    def exp_peer(distance):
        return lax.rem(side + distance, flight)

    gate_load = pltpu.make_async_copy(gate_hbm, gate_ref, local_sem.at[0])
    up_load = pltpu.make_async_copy(up_hbm, up_ref, local_sem.at[1])
    gate_load.start()
    up_load.start()

    barrier = pltpu.get_barrier_semaphore()

    def greet(distance, carry):
        pl.semaphore_signal(barrier, inc=1, device_id=(seq_peer(distance), side), device_id_type=MESH)
        return carry

    lax.fori_loop(1, count, greet, 0)
    for distance in range(1, flight):
        pl.semaphore_signal(barrier, inc=1, device_id=(me, exp_peer(distance)), device_id_type=MESH)
    pl.semaphore_wait(barrier, count - 1 + flight - 1)

    def remote(source, target, send_sem, arrive_sem, seq_index, exp_index):
        return pltpu.make_async_remote_copy(
            source, target, send_sem, arrive_sem, device_id=(seq_index, exp_index), device_id_type=MESH
        )

    rim_copy = remote(
        x_ref.at[pl.ds(length - 16, 16), :], rim_ref, rim_sem.at[0], rim_sem.at[1], seq_peer(1), side
    )

    @pl.when(me < count - 1)
    def _():
        rim_copy.start()

    above = lax.broadcasted_iota(jnp.int32, (length, length), 0) < lax.broadcasted_iota(
        jnp.int32, (length, length), 1
    )
    above = above.astype(jnp.float32).astype(jnp.bfloat16)
    slot = lax.broadcasted_iota(jnp.int32, (16, length), 0)
    for expert in range(flight):
        named = (routes_ref[pl.ds(0, 1), :] == expert).astype(jnp.float32)
        for choice in range(1, routes_ref.shape[0]):
            named = named + (routes_ref[pl.ds(choice, 1), :] == expert).astype(jnp.float32)
        named = jnp.broadcast_to(named, (16, length))
        rank = jnp.dot(named.astype(jnp.bfloat16), above, preferred_element_type=jnp.float32)
        taken = jnp.where(rank == slot.astype(jnp.float32), named, 0.0).astype(jnp.bfloat16)
        stage[expert, :, pl.ds(0, width)] = jnp.dot(
            taken, tokens_ref[...], preferred_element_type=jnp.float32
        ).astype(jnp.bfloat16)
        late = jnp.where(rank == (16 + (slot & 3)).astype(jnp.float32), named, 0.0)
        rest = jnp.zeros((16, quarter), jnp.float32)
        for part in range(4):
            mine = jnp.where((slot >> 2) == part, late, 0.0).astype(jnp.bfloat16)
            rest = rest + jnp.dot(
                mine, tokens_ref[:, pl.ds(part * quarter, quarter)], preferred_element_type=jnp.float32
            )
        stage[expert, :, pl.ds(width, quarter)] = rest.astype(jnp.bfloat16)

    def stage_copy(distance):
        return remote(
            stage.at[exp_peer(distance)], block_rows.at[me, side],
            pair_out.at[0, distance], pair_in.at[0, distance], me, exp_peer(distance),
        )

    def coef_copy(distance):
        return remote(
            parts_ref.at[side], parts_ref.at[side],
            pair_out.at[1, distance], pair_in.at[1, distance], me, exp_peer(distance),
        )

    for distance in range(1, flight):
        stage_copy(distance).start()
    block_rows[me, side] = stage[side]

    def step_tile(position, carry):
        lanes = pl.ds(pl.multiple_of(position * LANES, LANES), LANES)
        rows = pl.ds(pl.multiple_of(position * length, length), length)
        step_ref[rows, :] = softplus(raw_ref[:, lanes].astype(jnp.float32) + bias_ref[:, lanes])
        return carry

    lax.fori_loop(0, tiles, step_tile, 0)
    rate_rows(decay_ref, rate_ref)

    low = lax.rem(me, 4)
    plane = me // 4
    planes = count // 4
    across = me - low + lax.rem(low + 2, 4)
    beside = me + 1 - 2 * lax.rem(me, 2)
    far = across + 1 - 2 * lax.rem(across, 2)

    def row_copy(kind, source):
        target = (me + 4, me - 4, across, beside)[kind]
        return remote(
            block_rows.at[source], block_rows.at[source], rows_out.at[kind, source], rows_in.at[source], target, side
        )

    def arrived(source):
        row_copy(3, source).wait_recv()

    def pass_on(source, up, down, act):
        if up:
            pl.when(plane < planes - 1)(lambda: act(row_copy(0, source)))
        if down:
            pl.when(plane > 0)(lambda: act(row_copy(1, source)))
        act(row_copy(2, source))
        act(row_copy(3, source))

    def column_step(hop, act, wait):
        @pl.when(plane >= hop)
        def _():
            if wait:
                arrived(me - 4 * hop)
            pass_on(me - 4 * hop, True, False, act)

        @pl.when(plane + hop < planes)
        def _():
            if wait:
                arrived(me + 4 * hop)
            pass_on(me + 4 * hop, False, True, act)

    def across_step(hop, act, wait):
        if hop == 0:
            if wait:
                arrived(across)
            act(row_copy(3, across))
            return

        @pl.when(plane >= hop)
        def _():
            if wait:
                arrived(across - 4 * hop)
            act(row_copy(3, across - 4 * hop))

        @pl.when(plane + hop < planes)
        def _():
            if wait:
                arrived(across + 4 * hop)
            act(row_copy(3, across + 4 * hop))

    def start(copy):
        copy.start()

    def sent(copy):
        copy.wait_send()

    for distance in range(1, flight):
        stage_copy(distance).wait()
    pass_on(me, True, True, start)

    @pl.when(me > 0)
    def _():
        rim_copy.wait_recv()

    @pl.when(me == 0)
    def _():
        rim_ref[...] = jnp.zeros_like(rim_ref)

    def conv_tile(position, carry):
        lanes = pl.ds(pl.multiple_of(position * LANES, LANES), LANES)
        rows = pl.ds(pl.multiple_of(position * length, length), length)
        wide[pl.ds(0, 16), :] = rim_ref[:, lanes].astype(jnp.float32)
        wide[pl.ds(16, length), :] = x_ref[:, lanes].astype(jnp.float32)
        total = taps_ref[pl.ds(0, 1), lanes] * wide[pl.ds(17 - taps, length), :]
        for tap in range(1, taps):
            total = total + taps_ref[pl.ds(tap, 1), lanes] * wide[pl.ds(17 - taps + tap, length), :]
        conv = silu(total)
        conv_ref[rows, :] = conv
        drive_ref[rows, :] = step_ref[rows, :] * conv
        rounded[:, lanes] = conv.astype(jnp.bfloat16)
        return carry

    lax.fori_loop(0, tiles, conv_tile, 0)
    parts_ref[side] = jnp.dot(rounded[...], proj_ref[...], preferred_element_type=jnp.float32)
    for distance in range(1, flight):
        coef_copy(distance).start()
    if planes > 1:
        column_step(1, start, True)
    for distance in range(1, flight):
        coef_copy(distance).wait()
    coef = parts_ref[0]
    for other in range(1, flight):
        coef = coef + parts_ref[other]
    coef_ref[...] = coef
    splat_columns(coef_ref, 0, states, in_table)
    splat_columns(coef_ref, states, states, out_table)

    groups = tiles // SUB
    pair = 2 if groups % 2 == 0 else 1
    span = states // pair

    def lines(ref, group, offset, stride):
        return ref[pl.ds(group * SUB * stride + offset, SUB, stride=stride), :]

    def sweep(first, lead, begin, output):
        rates = [[lines(rate_ref, first + g, lead + n, states) for n in range(span)] for g in range(pair)]
        keep_total = lead == 0 and not output

        def block(turn, held):
            state = [list(held[g * span : (g + 1) * span]) for g in range(pair)]
            totals = list(held[pair * span :])
            for inner in range(4):
                t = turn * 4 + inner
                steps = [lines(step_ref, first + g, t, length) for g in range(pair)]
                drives = [lines(drive_ref, first + g, t, length) for g in range(pair)]
                if keep_total:
                    totals = [totals[g] + steps[g] for g in range(pair)]
                terms = [[None, None] for _ in range(pair)]
                for n in range(span):
                    row = in_table[pl.ds((lead + n) * length + t, 1), :]
                    if output:
                        out_row = out_table[pl.ds((lead + n) * length + t, 1), :]
                    for g in range(pair):
                        state[g][n] = jnp.exp2(rates[g][n] * steps[g]) * state[g][n] + row * drives[g]
                        if output:
                            term = out_row * state[g][n]
                            old = terms[g][n % 2]
                            terms[g][n % 2] = term if old is None else old + term
                if output:
                    for g in range(pair):
                        where = pl.ds((first + g) * SUB * length + t, SUB, stride=length)
                        part = terms[g][0] if span == 1 else terms[g][0] + terms[g][1]
                        sums[where, :] = part if lead == 0 else sums[where, :] + part
            return tuple(s for line in state for s in line) + tuple(totals)

        zeros = (jnp.zeros((SUB, LANES), jnp.float32),) * (pair if keep_total else 0)
        held = lax.fori_loop(0, length // 4, block, tuple(begin) + zeros)
        if keep_total:
            for g in range(pair):
                total_ref[pl.ds(pl.multiple_of((first + g) * SUB, SUB), SUB), :] = held[pair * span + g]
        return held

    events = [lambda hop=hop: column_step(hop, start, True) for hop in range(2, planes)]
    events += [lambda hop=hop: across_step(hop, start, True) for hop in range(planes)]
    units = [(first, lead) for first in range(0, groups, pair) for lead in range(0, states, span)]
    for number, (first, lead) in enumerate(units):
        zero = jnp.zeros((SUB, LANES), jnp.float32)
        held = sweep(first, lead, (zero,) * (pair * span), False)
        for g in range(pair):
            for n in range(span):
                end_ref[pl.ds((first + g) * SUB * states + lead + n, SUB, stride=states), :] = held[g * span + n]
        last = number == len(units) - 1
        for _ in range(len(events) if last else min(len(events), -(-planes // 2))):
            events.pop(0)()

    def lay_out(peer, carry):
        end_out[peer] = end_ref[pl.ds(peer * piece, piece), :].astype(jnp.bfloat16)
        total_out[peer] = total_ref[pl.ds(peer * piece // states, spread), :]
        return carry

    lax.fori_loop(0, count, lay_out, 0)

    def carry_copy(kind, distance):
        peer = seq_peer(distance)
        source = (end_out.at[peer], total_out.at[peer], leaving.at[peer])[kind]
        target = (got_end.at[me], got_total.at[me], entering.at[me])[kind]
        return remote(source, target, sends.at[kind, distance], arrivals.at[kind, distance], peer, side)

    def send_ends(distance, carry):
        carry_copy(0, distance).start()
        carry_copy(1, distance).start()
        return carry

    lax.fori_loop(1, count, send_ends, 0)
    got_end[me] = end_out[me]
    got_total[me] = total_out[me]

    def last_rows(turn, carry):
        arrived(lax.rem(beside, 4) + 4 * turn)
        arrived(lax.rem(far, 4) + 4 * turn)
        return carry

    lax.fori_loop(0, planes, last_rows, 0)

    small = 4 * count
    for half in range(flight):
        def lay_rows(source, carry):
            rows_ref[pl.ds(pl.multiple_of(source * 16, 16), 16), pl.ds(half * width, width)] = block_rows[
                source, half, :, pl.ds(0, width)
            ]
            return carry

        lax.fori_loop(0, count, lay_rows, 0)
        rest = block_rows[:, half, :, pl.ds(width, quarter)].reshape(16 * count, quarter)
        into = lax.broadcasted_iota(jnp.int32, (small, 16 * count), 0)
        out_of = lax.broadcasted_iota(jnp.int32, (small, 16 * count), 1)
        for part in range(4):
            pick = ((into >> 2) * 16 + part * 4 + (into & 3) == out_of).astype(jnp.float32).astype(jnp.bfloat16)
            rows_ref[pl.ds(16 * count, small), pl.ds(half * width + part * quarter, quarter)] = jnp.dot(
                pick, rest, preferred_element_type=jnp.float32
            ).astype(jnp.bfloat16)
    held_at = lax.broadcasted_iota(jnp.int32, order_ref.shape, 0)
    wanted = lax.broadcasted_iota(jnp.int32, order_ref.shape, 1)
    tail_at = held_at - 16 * count
    goes_to = jnp.where(
        held_at < 16 * count,
        (held_at >> 4) * CAP + (held_at & 15),
        (tail_at >> 2) * CAP + 16 + (tail_at & 3),
    )
    order_ref[...] = (goes_to == wanted).astype(jnp.float32).astype(jnp.bfloat16)
    gate_load.wait()
    up_load.wait()

    def expand(turn, carry):
        part = pl.ds(pl.multiple_of(turn * chunk, chunk), chunk)
        dims = (((1,), (1,)), ((), ()))
        gate = lax.dot_general(gate_ref[part, :], rows_ref[...], dims, preferred_element_type=jnp.float32)
        up = lax.dot_general(up_ref[part, :], rows_ref[...], dims, preferred_element_type=jnp.float32)
        value = (silu(gate) * up).astype(jnp.bfloat16)
        hidden_ref[part, :] = jnp.dot(value, order_ref[...], preferred_element_type=jnp.float32).astype(
            jnp.bfloat16
        )
        return carry

    turns = hidden_rows // chunk
    lax.fori_loop(0, turns // 2, expand, 0)

    def receive(distance, carry):
        carry_copy(0, distance).wait()
        carry_copy(1, distance).wait()
        return carry

    lax.fori_loop(1, count, receive, 0)
    own_rates = rate_ref[pl.ds(me * piece, piece), :]

    def join(source, state):
        leaving[source] = state.astype(jnp.bfloat16)
        totals = got_total[source]
        totals = jnp.broadcast_to(totals[:, None, :], (spread, piece // spread, LANES)).reshape(piece, LANES)
        return jnp.exp2(own_rates * totals) * state + got_end[source].astype(jnp.float32)

    lax.fori_loop(0, count, join, jnp.zeros((piece, LANES), jnp.float32))

    def send_back(distance, carry):
        carry_copy(2, distance).start()
        return carry

    lax.fori_loop(1, count, send_back, 0)
    entering[me] = leaving[me]
    lax.fori_loop(turns // 2, turns, expand, 0)

    def receive_back(distance, carry):
        carry_copy(2, distance).wait()
        return carry

    lax.fori_loop(1, count, receive_back, 0)

    def widen(source, carry):
        start_ref[pl.ds(source * piece, piece), :] = entering[source].astype(jnp.float32)
        return carry

    lax.fori_loop(0, count, widen, 0)

    def second(turn, carry):
        first = turn * pair
        for lead in range(0, states, span):
            begin = [lines(start_ref, first + g, lead + n, states) for g in range(pair) for n in range(span)]
            sweep(first, lead, begin, True)
        return carry

    lax.fori_loop(0, groups // pair, second, 0)

    def out_tile(position, carry):
        lanes = pl.ds(pl.multiple_of(position * LANES, LANES), LANES)
        rows = pl.ds(pl.multiple_of(position * length, length), length)
        result = sums[rows, :] + gain_ref[:, lanes] * conv_ref[rows, :]
        mixed_ref[:, lanes] = (result * silu(z_ref[:, lanes].astype(jnp.float32))).astype(jnp.bfloat16)
        return carry

    lax.fori_loop(0, tiles, out_tile, 0)

    @pl.when(me < count - 1)
    def _():
        rim_copy.wait_send()

    pass_on(me, True, True, sent)
    for hop in range(1, planes):
        column_step(hop, sent, False)
    for hop in range(planes):
        across_step(hop, sent, False)


def shards(
    inner_x,
    inner_z,
    step_raw,
    conv_weight,
    state_proj,
    step_bias,
    decay_log,
    skip_gain,
    moe_tokens,
    routes,
    gate_weight,
    up_weight,
):
    length, channels = inner_x.shape
    states = decay_log.shape[0]
    count, flight = lax.axis_size("seq"), lax.axis_size("exp")
    hidden_rows, features = gate_weight.shape[1:]
    width = moe_tokens.shape[1]
    tiles = channels // LANES
    piece = tiles * states // count
    spread = max(1, piece // states)
    slots = CAP * count
    whole, half = jnp.float32, jnp.bfloat16
    flat = pltpu.VMEM((tiles * length, LANES), whole)
    table = pltpu.VMEM((states * length, LANES), whole)
    held = pltpu.VMEM((tiles * states, LANES), whole)
    pieces = pltpu.VMEM((count, piece, LANES), half)
    totals = pltpu.VMEM((count, spread, LANES), whole)
    block = (16, width + width // 4)
    dma = pltpu.SemaphoreType.DMA
    in_vmem = pl.BlockSpec(memory_space=pltpu.VMEM)
    in_hbm = pl.BlockSpec(memory_space=pl.ANY)
    mixed, hidden = pl.pallas_call(
        functools.partial(mixer_kernel, count, flight),
        out_shape=(
            jax.ShapeDtypeStruct((length, channels), half),
            jax.ShapeDtypeStruct((hidden_rows, slots), half),
        ),
        in_specs=[in_vmem] * 10 + [in_hbm] * 2,
        out_specs=(in_vmem, in_vmem),
        scratch_shapes=[
            pltpu.VMEM((hidden_rows, features), half),
            pltpu.VMEM((hidden_rows, features), half),
            pltpu.VMEM((16, channels), half),
            pltpu.VMEM((length + 16, LANES), whole),
            pltpu.VMEM((length, channels), half),
            flat,
            flat,
            flat,
            pltpu.VMEM((flight, length, 2 * states), whole),
            pltpu.VMEM((length, 2 * states), whole),
            table,
            table,
            held,
            held,
            pltpu.VMEM((tiles, LANES), whole),
            pieces,
            totals,
            pieces,
            totals,
            pieces,
            pieces,
            held,
            flat,
            pltpu.VMEM((flight, *block), half),
            pltpu.VMEM((count, flight, *block), half),
            pltpu.VMEM((slots, features), half),
            pltpu.VMEM((slots, slots), half),
            dma((2,)),
            dma((2,)),
            dma((2, flight)),
            dma((2, flight)),
            dma((4, count)),
            dma((count,)),
            dma((3, count)),
            dma((3, count)),
        ],
        compiler_params=pltpu.CompilerParams(
            vmem_limit_bytes=VMEM_LIMIT, collective_id=0, has_side_effects=True
        ),
    )(
        inner_x, inner_z, step_raw, conv_weight, state_proj, step_bias[None, :], decay_log, skip_gain[None, :],
        moe_tokens, routes.T, gate_weight[0], up_weight[0],
    )
    return (mixed, hidden[None])


def solution(mesh):
    return jax.shard_map(
        shards,
        mesh=mesh,
        in_specs=(
            P("seq", "exp"),
            P("seq", "exp"),
            P("seq", "exp"),
            P(None, "exp"),
            P("exp", None),
            P("exp"),
            P(None, "exp"),
            P("exp"),
            P("seq", "exp"),
            P("seq", None),
            P("exp", "seq", None),
            P("exp", "seq", None),
        ),
        out_specs=(P("seq", "exp"), P("exp", "seq", None)),
        check_vma=False,
    )
```

time: 278 us -> 76.2 us (0.27)
  waiting for transfers between devices: 108 us -> 0 us
  other arithmetic: 64.9 us -> 0 us
  Pallas kernels: 0 us -> 62.1 us
  local copies, waits for them, and re-layouts: 63.6 us -> 12.9 us
  between operations: 14 us -> 0.65 us
  matrix products: 12.5 us -> 0 us
  blocking collectives: 6.73 us -> 0 us
  starting transfers between devices: 6.24 us -> 0 us
    all_gather x3 -> x0, waiting for transfers between devices: 104 us -> none  [the longest x2 87.5 us: carried_in(): pieces = jax.tree.map(lambda part: lax.all_gather(part, axis), value)]
    pallas_call x0 -> x1, Pallas kernels: none -> 62.1 us  [shards(): pl.pallas_call(functools.partial(mixer_kernel, count, flight), out_shape=...]
    slice x23 -> x0, local copies, waits for them, and re-layouts: 40.6 us -> none  [the longest x16 38.2 us: shards(): lax.scan(advance, incoming, (step_size, input_coef, output_coef, weighted...]
    reduce_sum x50 -> x0, other arithmetic: 27.4 us -> none  [the longest x48 19.5 us: advance(): return (state, jnp.sum(out_row[:, None] * state, axis=0))]
    select_n x15 -> x0, other arithmetic: 18.7 us -> none  [turn(): jnp.where(position < mine, new, old)]
    dot_general x4 -> x0, matrix products: 12.5 us -> none  [the longest x1 5.95 us: expand_rows(): lax.dot_general(gate_matrix, slot_rows, dims, preferred_element_type=jnp....]
    dynamic_update_slice x16 -> x0, local copies, waits for them, and re-layouts: 10.6 us -> none  [shards(): lax.scan(advance, incoming, (step_size, input_coef, output_coef, weighted...]
    unnamed x21, local copies, waits for them, and re-layouts: 6.12 us -> 12.9 us
  transfers between devices with their start and end apart: 5 -> 0, of which waited for: 4 -> 0; matrix products, arithmetic and copies ran while one was open for 16% -> 0% of each run, Pallas kernels for 0% -> 0%
where the time goes in v2:
time: 76.2 us; the launch traced here: 75.7 us
  Pallas kernels  62.1 us (81%)
  local copies, waits for them, and re-layouts  12.9 us (17%)
    pallas_call x1, Pallas kernels, shards(): pl.pallas_call(functools.partial(mixer_kernel, count, flight), out_shape=...  62.1 us
    unnamed x21, local copies, waits for them, and re-layouts  12.9 us

profile of v2, /device:TPU:0, one launch (start us, length us, event | category | flops | bytes accessed | tf_op | source)
XLA Modules:
  0.0 75.7 jit_solution(17709426711466190176)
XLA Ops:
  0.6 2.3 %copy.14.proj_ref = bf16[4096,32]{1,0:T(8,128)(2,1)} copy(bf16[4096,32]{0,1:T(8,128)(2,1)} %param.16) | data formatting | bytes 524288 | tf_op args[4]
  2.9 0.0 copy-start
  2.9 1.2 %copy-done = bf16[128,4096]{1,0:T(8,128)(2,1)S(1)} copy-done((bf16[128,4096]{1,0:T(8,128)(2,1)S(1)}, bf16[128,4096]{1,0:T(8,128)(2,1)}, u32[]{:S(2)}) %copy-start) | copy-done | bytes 1048600
  4.1 0.0 copy-start.1
  4.1 1.2 %copy-done.1 = bf16[128,4096]{1,0:T(8,128)(2,1)S(1)} copy-done((bf16[128,4096]{1,0:T(8,128)(2,1)S(1)}, bf16[128,4096]{1,0:T(8,128)(2,1)}, u32[]{:S(2)}) %copy-start.1) | copy-done | bytes 1048600
  5.3 0.0 copy-start.2
  5.3 1.2 %copy-done.2 = bf16[128,4096]{1,0:T(8,128)(2,1)S(1)} copy-done((bf16[128,4096]{1,0:T(8,128)(2,1)S(1)}, bf16[128,4096]{1,0:T(8,128)(2,1)}, u32[]{:S(2)}) %copy-start.2) | copy-done | bytes 1048600
  6.6 0.0 copy-start.3
  6.6 1.0 %copy-done.3 = bf16[128,2048]{1,0:T(8,128)(2,1)S(1)} copy-done((bf16[128,2048]{1,0:T(8,128)(2,1)S(1)}, bf16[128,2048]{1,0:T(8,128)(2,1)}, u32[]{:S(2)}) %copy-start.3) | copy-done | bytes 524312
  7.6 0.0 copy-start.4
  7.6 0.9 %copy-done.4 = f32[16,4096]{1,0:T(8,128)S(1)} copy-done((f32[16,4096]{1,0:T(8,128)S(1)}, f32[16,4096]{1,0:T(8,128)}, u32[]{:S(2)}) %copy-start.4) | copy-done | bytes 262168
  8.6 0.0 copy-start.5
  8.6 0.8 %copy-done.5 = f32[4,4096]{1,0:T(4,128)S(1)} copy-done((f32[4,4096]{1,0:T(4,128)S(1)}, f32[4,4096]{1,0:T(4,128)}, u32[]{:S(2)}) %copy-start.5) | copy-done | bytes 65560
  9.4 0.0 copy-start.6
  9.4 0.7 copy-done.6
  10.1 0.0 copy-start.7
  10.1 0.7 copy-done.7
  10.8 0.0 copy-start.8
  10.8 0.7 copy-done.8
  11.5 62.1 %shard_map.131 = (bf16[128,4096]{1,0:T(8,128)(2,1)S(1)}, bf16[768,320]{1,0:T(8,128)(2,1)S(1)}) custom-call(bf16[128,4096]{1,0:T(8,128)(2,1)S(1)} %copy-done, bf16[128,4096]{1,0:T(8,128)(2,1)S(1)} %copy-done.1, bf16[128,4096]{1,0:T(8,128)(2,1)S(1)} %copy-done.2, f32[4,4096]{1,0:T(4,128)S(1)} %copy-done.5, bf16[4096,32]{1,0:T(8,128)(2,1)} %copy.14.proj_ref, ...), custom_call_target="tpu_custom_call" | custom-call | tf_op jit(solution)/shard_map/pallas_call | solution.py:484
  73.7 1.0 %copy.15 = bf16[1,768,320]{1,2,0:T(8,128)(2,1)} copy(bf16[1,768,320]{2,1,0:T(8,128)(2,1)S(1)} %bitcast.6) | data formatting | bytes 983040
  74.7 1.0 %copy.17 = bf16[128,4096]{1,0:T(8,128)(2,1)} copy(bf16[128,4096]{1,0:T(8,128)(2,1)S(1)} %get-tuple-element.10) | data formatting | bytes 2097152
Async XLA Ops:
  2.9 1.2 %copy-start = (bf16[128,4096]{1,0:T(8,128)(2,1)S(1)}, bf16[128,4096]{1,0:T(8,128)(2,1)}, u32[]{:S(2)}) copy-start(bf16[128,4096]{1,0:T(8,128)(2,1)} %x_ref.1) | copy-start | bytes 3145732
  4.1 1.2 %copy-start.1 = (bf16[128,4096]{1,0:T(8,128)(2,1)S(1)}, bf16[128,4096]{1,0:T(8,128)(2,1)}, u32[]{:S(2)}) copy-start(bf16[128,4096]{1,0:T(8,128)(2,1)} %z_ref.1) | copy-start | bytes 3145732
  5.3 1.2 %copy-start.2 = (bf16[128,4096]{1,0:T(8,128)(2,1)S(1)}, bf16[128,4096]{1,0:T(8,128)(2,1)}, u32[]{:S(2)}) copy-start(bf16[128,4096]{1,0:T(8,128)(2,1)} %raw_ref.1) | copy-start | bytes 3145732
  6.6 1.0 %copy-start.3 = (bf16[128,2048]{1,0:T(8,128)(2,1)S(1)}, bf16[128,2048]{1,0:T(8,128)(2,1)}, u32[]{:S(2)}) copy-start(bf16[128,2048]{1,0:T(8,128)(2,1)} %tokens_ref.1) | copy-start | bytes 1572868
  7.6 0.9 %copy-start.4 = (f32[16,4096]{1,0:T(8,128)S(1)}, f32[16,4096]{1,0:T(8,128)}, u32[]{:S(2)}) copy-start(f32[16,4096]{1,0:T(8,128)} %decay_ref.1) | copy-start | bytes 786436
  8.6 0.8 %copy-start.5 = (f32[4,4096]{1,0:T(4,128)S(1)}, f32[4,4096]{1,0:T(4,128)}, u32[]{:S(2)}) copy-start(f32[4,4096]{1,0:T(4,128)} %taps_ref.1) | copy-start | bytes 196612
  9.4 0.7 copy-start.6
  10.1 0.7 copy-start.7
  10.8 0.7 copy-start.8

commit v3 on v2

--- a/solution.py
+++ b/solution.py
@@ -12,7 +12,7 @@
 SUB = 8
 LOG2E = 1.4426950408889634
 MESH = pl.DeviceIdType.MESH
-VMEM_LIMIT = 48 * 1024 * 1024
+VMEM_LIMIT = 60 * 1024 * 1024
 
 
 def silu(value):
@@ -47,8 +47,9 @@
 
 
 def mixer_kernel(
-    count, flight, x_ref, z_ref, raw_ref, taps_ref, proj_ref, bias_ref, decay_ref, gain_ref, tokens_ref, routes_ref,
+    count, flight, x_hbm, z_hbm, raw_hbm, taps_hbm, proj_hbm, bias_hbm, decay_hbm, gain_hbm, tokens_hbm, routes_hbm,
     gate_hbm, up_hbm, mixed_ref, hidden_ref,
+    x_ref, z_ref, raw_ref, taps_ref, proj_ref, bias_ref, decay_ref, gain_ref, tokens_ref, routes_ref,
     gate_ref, up_ref, rim_ref, wide, rounded, conv_ref, step_ref, drive_ref, parts_ref, coef_ref, in_table, out_table,
     rate_ref, end_ref, total_ref, end_out, total_out, got_end, got_total, leaving, entering, start_ref, sums,
     stage, block_rows, rows_ref, order_ref,
@@ -72,10 +73,18 @@
     def exp_peer(distance):
         return lax.rem(side + distance, flight)
 
-    gate_load = pltpu.make_async_copy(gate_hbm, gate_ref, local_sem.at[0])
-    up_load = pltpu.make_async_copy(up_hbm, up_ref, local_sem.at[1])
-    gate_load.start()
-    up_load.start()
+    loads = [
+        pltpu.make_async_copy(source, target, local_sem.at[number])
+        for number, (source, target) in enumerate(
+            (
+                (routes_hbm, routes_ref), (tokens_hbm, tokens_ref), (raw_hbm, raw_ref), (bias_hbm, bias_ref),
+                (decay_hbm, decay_ref), (x_hbm, x_ref), (taps_hbm, taps_ref), (proj_hbm, proj_ref),
+                (z_hbm, z_ref), (gain_hbm, gain_ref), (gate_hbm, gate_ref), (up_hbm, up_ref),
+            )
+        )
+    ]
+    for load in loads:
+        load.start()
 
     barrier = pltpu.get_barrier_semaphore()
 
@@ -94,7 +103,7 @@
         )
 
     rim_copy = remote(
-        x_ref.at[pl.ds(length - 16, 16), :], rim_ref, rim_sem.at[0], rim_sem.at[1], seq_peer(1), side
+        x_hbm.at[pl.ds(length - 16, 16), :], rim_ref, rim_sem.at[0], rim_sem.at[1], seq_peer(1), side
     )
 
     @pl.when(me < count - 1)
@@ -106,6 +115,8 @@
     )
     above = above.astype(jnp.float32).astype(jnp.bfloat16)
     slot = lax.broadcasted_iota(jnp.int32, (16, length), 0)
+    for load in loads[:2]:
+        load.wait()
     for expert in range(flight):
         named = (routes_ref[pl.ds(0, 1), :] == expert).astype(jnp.float32)
         for choice in range(1, routes_ref.shape[0]):
@@ -147,8 +158,9 @@
         step_ref[rows, :] = softplus(raw_ref[:, lanes].astype(jnp.float32) + bias_ref[:, lanes])
         return carry
 
-    lax.fori_loop(0, tiles, step_tile, 0)
-    rate_rows(decay_ref, rate_ref)
+    for load in loads[2:4]:
+        load.wait()
+    lax.fori_loop(0, tiles // 2, step_tile, 0)
 
     low = lax.rem(me, 4)
     plane = me // 4
@@ -215,6 +227,20 @@
     for distance in range(1, flight):
         stage_copy(distance).wait()
     pass_on(me, True, True, start)
+    lax.fori_loop(tiles // 2, tiles, step_tile, 0)
+    loads[4].wait()
+    rate_rows(decay_ref, rate_ref)
+    held_at = lax.broadcasted_iota(jnp.int32, order_ref.shape, 1)
+    wanted = lax.broadcasted_iota(jnp.int32, order_ref.shape, 0)
+    tail_at = held_at - 16 * count
+    goes_to = jnp.where(
+        held_at < 16 * count,
+        (held_at >> 4) * CAP + (held_at & 15),
+        (tail_at >> 2) * CAP + 16 + (tail_at & 3),
+    )
+    order_ref[...] = (goes_to == wanted).astype(jnp.float32).astype(jnp.bfloat16)
+    for load in loads[5:8]:
+        load.wait()
 
     @pl.when(me > 0)
     def _():
@@ -238,12 +264,16 @@
         rounded[:, lanes] = conv.astype(jnp.bfloat16)
         return carry
 
-    lax.fori_loop(0, tiles, conv_tile, 0)
-    parts_ref[side] = jnp.dot(rounded[...], proj_ref[...], preferred_element_type=jnp.float32)
+    lax.fori_loop(0, tiles // 2, conv_tile, 0)
+    if planes > 1:
+        column_step(1, start, True)
+    lax.fori_loop(tiles // 2, tiles, conv_tile, 0)
+    dims = (((1,), (1,)), ((), ()))
+    parts_ref[side] = lax.dot_general(rounded[...], proj_ref[...], dims, preferred_element_type=jnp.float32)
     for distance in range(1, flight):
         coef_copy(distance).start()
-    if planes > 1:
-        column_step(1, start, True)
+    if planes > 2:
+        column_step(2, start, True)
     for distance in range(1, flight):
         coef_copy(distance).wait()
     coef = parts_ref[0]
@@ -298,7 +328,28 @@
                 total_ref[pl.ds(pl.multiple_of((first + g) * SUB, SUB), SUB), :] = held[pair * span + g]
         return held
 
-    events = [lambda hop=hop: column_step(hop, start, True) for hop in range(2, planes)]
+    def carry_copy(kind, distance):
+        peer = seq_peer(distance)
+        source = (end_out.at[peer], total_out.at[peer], leaving.at[peer])[kind]
+        target = (got_end.at[me], got_total.at[me], entering.at[me])[kind]
+        return remote(source, target, sends.at[kind, distance], arrivals.at[kind, distance], peer, side)
+
+    def send_ends(begin, stop):
+        def one(peer, carry):
+            end_out[peer] = end_ref[pl.ds(peer * piece, piece), :].astype(jnp.bfloat16)
+            total_out[peer] = total_ref[pl.ds(peer * piece // states, spread), :]
+
+            @pl.when(peer != me)
+            def _():
+                distance = lax.rem(peer - me + count, count)
+                carry_copy(0, distance).start()
+                carry_copy(1, distance).start()
+
+            return carry
+
+        lax.fori_loop(begin, stop, one, 0)
+
+    events = [lambda hop=hop: column_step(hop, start, True) for hop in range(3, planes)]
     events += [lambda hop=hop: across_step(hop, start, True) for hop in range(planes)]
     units = [(first, lead) for first in range(0, groups, pair) for lead in range(0, states, span)]
     for number, (first, lead) in enumerate(units):
@@ -307,31 +358,14 @@
         for g in range(pair):
             for n in range(span):
                 end_ref[pl.ds((first + g) * SUB * states + lead + n, SUB, stride=states), :] = held[g * span + n]
-        last = number == len(units) - 1
-        for _ in range(len(events) if last else min(len(events), -(-planes // 2))):
+        if lead + span == states:
+            send_ends(count * first // groups, count * (first + pair) // groups)
+        for _ in range(0 if number == len(units) - 1 else min(len(events), 1 + (number == 0))):
             events.pop(0)()
-
-    def lay_out(peer, carry):
-        end_out[peer] = end_ref[pl.ds(peer * piece, piece), :].astype(jnp.bfloat16)
-        total_out[peer] = total_ref[pl.ds(peer * piece // states, spread), :]
-        return carry
-
-    lax.fori_loop(0, count, lay_out, 0)
-
-    def carry_copy(kind, distance):
-        peer = seq_peer(distance)
-        source = (end_out.at[peer], total_out.at[peer], leaving.at[peer])[kind]
-        target = (got_end.at[me], got_total.at[me], entering.at[me])[kind]
-        return remote(source, target, sends.at[kind, distance], arrivals.at[kind, distance], peer, side)
-
-    def send_ends(distance, carry):
-        carry_copy(0, distance).start()
-        carry_copy(1, distance).start()
-        return carry
-
-    lax.fori_loop(1, count, send_ends, 0)
     got_end[me] = end_out[me]
     got_total[me] = total_out[me]
+    for event in events:
+        event()
 
     def last_rows(turn, carry):
         arrived(lax.rem(beside, 4) + 4 * turn)
@@ -357,32 +391,6 @@
             rows_ref[pl.ds(16 * count, small), pl.ds(half * width + part * quarter, quarter)] = jnp.dot(
                 pick, rest, preferred_element_type=jnp.float32
             ).astype(jnp.bfloat16)
-    held_at = lax.broadcasted_iota(jnp.int32, order_ref.shape, 0)
-    wanted = lax.broadcasted_iota(jnp.int32, order_ref.shape, 1)
-    tail_at = held_at - 16 * count
-    goes_to = jnp.where(
-        held_at < 16 * count,
-        (held_at >> 4) * CAP + (held_at & 15),
-        (tail_at >> 2) * CAP + 16 + (tail_at & 3),
-    )
-    order_ref[...] = (goes_to == wanted).astype(jnp.float32).astype(jnp.bfloat16)
-    gate_load.wait()
-    up_load.wait()
-
-    def expand(turn, carry):
-        part = pl.ds(pl.multiple_of(turn * chunk, chunk), chunk)
-        dims = (((1,), (1,)), ((), ()))
-        gate = lax.dot_general(gate_ref[part, :], rows_ref[...], dims, preferred_element_type=jnp.float32)
-        up = lax.dot_general(up_ref[part, :], rows_ref[...], dims, preferred_element_type=jnp.float32)
-        value = (silu(gate) * up).astype(jnp.bfloat16)
-        hidden_ref[part, :] = jnp.dot(value, order_ref[...], preferred_element_type=jnp.float32).astype(
-            jnp.bfloat16
-        )
-        return carry
-
-    turns = hidden_rows // chunk
-    lax.fori_loop(0, turns // 2, expand, 0)
-
     def receive(distance, carry):
         carry_copy(0, distance).wait()
         carry_copy(1, distance).wait()
@@ -397,7 +405,7 @@
         totals = jnp.broadcast_to(totals[:, None, :], (spread, piece // spread, LANES)).reshape(piece, LANES)
         return jnp.exp2(own_rates * totals) * state + got_end[source].astype(jnp.float32)
 
-    lax.fori_loop(0, count, join, jnp.zeros((piece, LANES), jnp.float32))
+    lax.fori_loop(0, count, join, jnp.zeros((piece, LANES), jnp.float32), unroll=4)
 
     def send_back(distance, carry):
         carry_copy(2, distance).start()
@@ -405,7 +413,16 @@
 
     lax.fori_loop(1, count, send_back, 0)
     entering[me] = leaving[me]
-    lax.fori_loop(turns // 2, turns, expand, 0)
+    for load in loads[8:]:
+        load.wait()
+    for turn in range(hidden_rows // chunk):
+        part = pl.ds(turn * chunk, chunk)
+        gate = lax.dot_general(rows_ref[...], gate_ref[part, :], dims, preferred_element_type=jnp.float32)
+        up = lax.dot_general(rows_ref[...], up_ref[part, :], dims, preferred_element_type=jnp.float32)
+        value = (silu(gate) * up).astype(jnp.bfloat16)
+        hidden_ref[:, part] = jnp.dot(order_ref[...], value, preferred_element_type=jnp.float32).astype(
+            jnp.bfloat16
+        )
 
     def receive_back(distance, carry):
         carry_copy(2, distance).wait()
@@ -480,16 +497,21 @@
     block = (16, width + width // 4)
     dma = pltpu.SemaphoreType.DMA
     in_vmem = pl.BlockSpec(memory_space=pltpu.VMEM)
-    in_hbm = pl.BlockSpec(memory_space=pl.ANY)
+    in_hbm = pl.BlockSpec(memory_space=pltpu.HBM)
+    operands = (
+        inner_x, inner_z, step_raw, conv_weight, state_proj.T, step_bias[None, :], decay_log, skip_gain[None, :],
+        moe_tokens, routes.T,
+    )
     mixed, hidden = pl.pallas_call(
         functools.partial(mixer_kernel, count, flight),
         out_shape=(
             jax.ShapeDtypeStruct((length, channels), half),
-            jax.ShapeDtypeStruct((hidden_rows, slots), half),
+            jax.ShapeDtypeStruct((slots, hidden_rows), half),
         ),
-        in_specs=[in_vmem] * 10 + [in_hbm] * 2,
+        in_specs=[in_hbm] * 12,
         out_specs=(in_vmem, in_vmem),
         scratch_shapes=[
+            *(pltpu.VMEM(operand.shape, operand.dtype) for operand in operands),
             pltpu.VMEM((hidden_rows, features), half),
             pltpu.VMEM((hidden_rows, features), half),
             pltpu.VMEM((16, channels), half),
@@ -517,7 +539,7 @@
             pltpu.VMEM((count, flight, *block), half),
             pltpu.VMEM((slots, features), half),
             pltpu.VMEM((slots, slots), half),
-            dma((2,)),
+            dma((12,)),
             dma((2,)),
             dma((2, flight)),
             dma((2, flight)),
@@ -529,11 +551,8 @@
         compiler_params=pltpu.CompilerParams(
             vmem_limit_bytes=VMEM_LIMIT, collective_id=0, has_side_effects=True
         ),
-    )(
-        inner_x, inner_z, step_raw, conv_weight, state_proj, step_bias[None, :], decay_log, skip_gain[None, :],
-        moe_tokens, routes.T, gate_weight[0], up_weight[0],
-    )
-    return (mixed, hidden[None])
+    )(*operands, gate_weight[0], up_weight[0])
+    return (mixed, hidden.T[None])
 
 
 def solution(mesh):

time: 76.2 us -> 66.5 us (0.87)
  local copies, waits for them, and re-layouts: 12.9 us -> 4.13 us
    unnamed x21 -> x2, local copies, waits for them, and re-layouts: 12.9 us -> 4.13 us
where the time goes in v3:
time: 66.5 us; the launch traced here: 66.3 us
  Pallas kernels  61.5 us (92%)
  local copies, waits for them, and re-layouts  4.13 us (6%)
    pallas_call x1, Pallas kernels, shards(): pl.pallas_call(functools.partial(mixer_kernel, count, flight), out_shape=...  61.5 us
    unnamed x2, local copies, waits for them, and re-layouts  4.13 us

profile of v3, /device:TPU:0, one launch (start us, length us, event | category | flops | bytes accessed | tf_op | source)
XLA Modules:
  0.0 66.3 jit_solution(6064091278261532668)
XLA Ops:
  0.6 61.5 %shard_map.131 = (bf16[128,4096]{1,0:T(8,128)(2,1)}, bf16[320,768]{1,0:T(8,128)(2,1)}) custom-call(bf16[128,4096]{1,0:T(8,128)(2,1)} %x_hbm.1, bf16[128,4096]{1,0:T(8,128)(2,1)} %z_hbm.1, bf16[128,4096]{1,0:T(8,128)(2,1)} %raw_hbm.1, f32[4,4096]{1,0:T(4,128)} %taps_hbm.1, bf16[32,4096]{1,0:T(8,128)(2,1)} %bitcast.12, f32[1,4096]{1,0:T(1,128)} %bitcast.13, ...), custom_call_target="tpu_custom_call" | custom-call | tf_op jit(solution)/shard_map/pallas_call | solution.py:505
  62.2 2.3 %copy.16 = bf16[128,4096]{1,0:T(8,128)(2,1)} copy(bf16[128,4096]{1,0:T(8,128)(2,1)} %get-tuple-element.8) | data formatting | bytes 2097152
  64.4 1.8 %copy.17 = bf16[1,768,320]{1,2,0:T(8,128)(2,1)} copy(bf16[1,768,320]{1,2,0:T(8,128)(2,1)} %bitcast.11) | data formatting | bytes 983040

commit v4 on v3

--- a/solution.py
+++ b/solution.py
@@ -8,6 +8,7 @@
 from jax.sharding import PartitionSpec as P
 
 CAP = 20
+TURN = 8
 LANES = 128
 SUB = 8
 LOG2E = 1.4426950408889634
@@ -51,7 +52,7 @@
     gate_hbm, up_hbm, mixed_ref, hidden_ref,
     x_ref, z_ref, raw_ref, taps_ref, proj_ref, bias_ref, decay_ref, gain_ref, tokens_ref, routes_ref,
     gate_ref, up_ref, rim_ref, wide, rounded, conv_ref, step_ref, drive_ref, parts_ref, coef_ref, in_table, out_table,
-    rate_ref, end_ref, total_ref, end_out, total_out, got_end, got_total, leaving, entering, start_ref, sums,
+    rate_ref, end_ref, total_ref, end_out, got_end, leaving, entering, start_ref, sums,
     stage, block_rows, rows_ref, order_ref,
     local_sem, rim_sem, pair_out, pair_in, rows_out, rows_in, sends, arrivals,
 ):
@@ -62,7 +63,9 @@
     quarter = width // 4
     tiles = channels // LANES
     piece = tiles * states // count
-    spread = got_total.shape[1]
+    spread = max(1, piece // states)
+    lead_rows = -(-piece // 16) * 16
+    extra_rows = end_out.shape[1] - lead_rows
     hidden_rows = gate_ref.shape[0]
     chunk = 256 if hidden_rows % 256 == 0 else hidden_rows
     me, side = lax.axis_index("seq"), lax.axis_index("exp")
@@ -297,8 +300,8 @@
         def block(turn, held):
             state = [list(held[g * span : (g + 1) * span]) for g in range(pair)]
             totals = list(held[pair * span :])
-            for inner in range(4):
-                t = turn * 4 + inner
+            for inner in range(TURN):
+                t = turn * TURN + inner
                 steps = [lines(step_ref, first + g, t, length) for g in range(pair)]
                 drives = [lines(drive_ref, first + g, t, length) for g in range(pair)]
                 if keep_total:
@@ -322,7 +325,7 @@
             return tuple(s for line in state for s in line) + tuple(totals)
 
         zeros = (jnp.zeros((SUB, LANES), jnp.float32),) * (pair if keep_total else 0)
-        held = lax.fori_loop(0, length // 4, block, tuple(begin) + zeros)
+        held = lax.fori_loop(0, length // TURN, block, tuple(begin) + zeros)
         if keep_total:
             for g in range(pair):
                 total_ref[pl.ds(pl.multiple_of((first + g) * SUB, SUB), SUB), :] = held[pair * span + g]
@@ -330,20 +333,27 @@
 
     def carry_copy(kind, distance):
         peer = seq_peer(distance)
-        source = (end_out.at[peer], total_out.at[peer], leaving.at[peer])[kind]
-        target = (got_end.at[me], got_total.at[me], entering.at[me])[kind]
+        source = (end_out.at[peer], leaving.at[peer])[kind]
+        target = (got_end.at[me], entering.at[me])[kind]
         return remote(source, target, sends.at[kind, distance], arrivals.at[kind, distance], peer, side)
 
     def send_ends(begin, stop):
         def one(peer, carry):
-            end_out[peer] = end_ref[pl.ds(peer * piece, piece), :].astype(jnp.bfloat16)
-            total_out[peer] = total_ref[pl.ds(peer * piece // states, spread), :]
+            end_out[peer, pl.ds(0, piece), :] = end_ref[pl.ds(peer * piece, piece), :].astype(jnp.bfloat16)
+            line = lax.broadcasted_iota(jnp.int32, (extra_rows, LANES), 0)
+            rest = jnp.zeros((extra_rows, LANES), jnp.float32)
+            for row in range(spread):
+                total = total_ref[pl.ds(peer * piece // states + row, 1), :]
+                for part in range(3):
+                    top = total.astype(jnp.bfloat16).astype(jnp.float32)
+                    rest = jnp.where(line == part * spread + row, top, rest)
+                    total = total - top
+            end_out[peer, pl.ds(lead_rows, extra_rows), :] = rest.astype(jnp.bfloat16)
 
             @pl.when(peer != me)
             def _():
                 distance = lax.rem(peer - me + count, count)
                 carry_copy(0, distance).start()
-                carry_copy(1, distance).start()
 
             return carry
 
@@ -363,7 +373,6 @@
         for _ in range(0 if number == len(units) - 1 else min(len(events), 1 + (number == 0))):
             events.pop(0)()
     got_end[me] = end_out[me]
-    got_total[me] = total_out[me]
     for event in events:
         event()
 
@@ -393,25 +402,31 @@
             ).astype(jnp.bfloat16)
     def receive(distance, carry):
         carry_copy(0, distance).wait()
-        carry_copy(1, distance).wait()
         return carry
 
     lax.fori_loop(1, count, receive, 0)
     own_rates = rate_ref[pl.ds(me * piece, piece), :]
 
+    column = lax.broadcasted_iota(jnp.int32, (piece, extra_rows), 1)
+    kept = lax.broadcasted_iota(jnp.int32, (piece, extra_rows), 0) // (piece // spread)
+    adds = jnp.zeros((piece, extra_rows), jnp.float32)
+    for part in range(3):
+        adds = adds + (column == part * spread + kept).astype(jnp.float32)
+    adds = adds.astype(jnp.bfloat16)
+
     def join(source, state):
         leaving[source] = state.astype(jnp.bfloat16)
-        totals = got_total[source]
-        totals = jnp.broadcast_to(totals[:, None, :], (spread, piece // spread, LANES)).reshape(piece, LANES)
-        return jnp.exp2(own_rates * totals) * state + got_end[source].astype(jnp.float32)
+
+        @pl.when(source != me)
+        def _():
+            carry_copy(1, lax.rem(source - me + count, count)).start()
+
+        totals = jnp.dot(
+            adds, got_end[source, pl.ds(lead_rows, extra_rows), :], preferred_element_type=jnp.float32
+        )
+        return jnp.exp2(own_rates * totals) * state + got_end[source, pl.ds(0, piece), :].astype(jnp.float32)
 
     lax.fori_loop(0, count, join, jnp.zeros((piece, LANES), jnp.float32), unroll=4)
-
-    def send_back(distance, carry):
-        carry_copy(2, distance).start()
-        return carry
-
-    lax.fori_loop(1, count, send_back, 0)
     entering[me] = leaving[me]
     for load in loads[8:]:
         load.wait()
@@ -425,7 +440,7 @@
         )
 
     def receive_back(distance, carry):
-        carry_copy(2, distance).wait()
+        carry_copy(1, distance).wait()
         return carry
 
     lax.fori_loop(1, count, receive_back, 0)
@@ -463,6 +478,19 @@
         column_step(hop, sent, False)
     for hop in range(planes):
         across_step(hop, sent, False)
+
+
+def hand_out(mixed_ref, hidden_ref, mixed_out, hidden_out, sems):
+    copies = []
+    for source, target in ((mixed_ref, mixed_out), (hidden_ref, hidden_out)):
+        share = source.shape[0] // 4
+        for part in range(4):
+            rows = pl.ds(part * share, share)
+            copies.append(pltpu.make_async_copy(source.at[rows, :], target.at[rows, :], sems.at[len(copies)]))
+    for copy in copies:
+        copy.start()
+    for copy in copies:
+        copy.wait()
 
 
 def shards(
@@ -493,7 +521,7 @@
     table = pltpu.VMEM((states * length, LANES), whole)
     held = pltpu.VMEM((tiles * states, LANES), whole)
     pieces = pltpu.VMEM((count, piece, LANES), half)
-    totals = pltpu.VMEM((count, spread, LANES), whole)
+    ends = pltpu.VMEM((count, -(-piece // 16) * 16 + -(-3 * spread // 16) * 16, LANES), half)
     block = (16, width + width // 4)
     dma = pltpu.SemaphoreType.DMA
     in_vmem = pl.BlockSpec(memory_space=pltpu.VMEM)
@@ -527,10 +555,8 @@
             held,
             held,
             pltpu.VMEM((tiles, LANES), whole),
-            pieces,
-            totals,
-            pieces,
-            totals,
+            ends,
+            ends,
             pieces,
             pieces,
             held,
@@ -545,13 +571,24 @@
             dma((2, flight)),
             dma((4, count)),
             dma((count,)),
-            dma((3, count)),
-            dma((3, count)),
+            dma((2, count)),
+            dma((2, count)),
         ],
         compiler_params=pltpu.CompilerParams(
             vmem_limit_bytes=VMEM_LIMIT, collective_id=0, has_side_effects=True
         ),
     )(*operands, gate_weight[0], up_weight[0])
+    mixed, hidden = pl.pallas_call(
+        hand_out,
+        out_shape=(
+            jax.ShapeDtypeStruct((length, channels), half),
+            jax.ShapeDtypeStruct((slots, hidden_rows), half),
+        ),
+        in_specs=[in_hbm] * 2,
+        out_specs=(in_hbm, in_hbm),
+        scratch_shapes=[dma((8,))],
+        compiler_params=pltpu.CompilerParams(vmem_limit_bytes=VMEM_LIMIT),
+    )(mixed, hidden)
     return (mixed, hidden.T[None])
 
 

time: 66.5 us -> 109 us (1.64)
  Pallas kernels: 61.5 us -> 108 us
  local copies, waits for them, and re-layouts: 4.13 us -> 0 us
    pallas_call x0 -> x1, Pallas kernels: none -> 47.8 us  [shards(): pl.pallas_call(hand_out, out_shape=(jax.ShapeDtypeStruct((length, channel...]
    unnamed x2 -> x0, local copies, waits for them, and re-layouts: 4.13 us -> none
    pallas_call x1, Pallas kernels: 61.5 us -> 60.2 us  [shards(): pl.pallas_call(functools.partial(mixer_kernel, count, flight), out_shape=...]
where the time goes in v4:
time: 109 us
  Pallas kernels  108 us (99%)
    pallas_call x1, Pallas kernels, shards(): pl.pallas_call(functools.partial(mixer_kernel, count, flight), out_shape=...  60.2 us
    pallas_call x1, Pallas kernels, shards(): pl.pallas_call(hand_out, out_shape=(jax.ShapeDtypeStruct((length, channel...  47.8 us

profile of v4, /device:TPU:0, one launch (start us, length us, event | category | flops | bytes accessed | tf_op | source)
XLA Modules:
  0.0 108.6 jit_solution(5335525481985637516)
XLA Ops:
  0.6 60.2 %shard_map.131 = (bf16[128,4096]{1,0:T(8,128)(2,1)}, bf16[320,768]{1,0:T(8,128)(2,1)}) custom-call(bf16[128,4096]{1,0:T(8,128)(2,1)} %x_hbm.1, bf16[128,4096]{1,0:T(8,128)(2,1)} %z_hbm.1, bf16[128,4096]{1,0:T(8,128)(2,1)} %raw_hbm.1, f32[4,4096]{1,0:T(4,128)} %taps_hbm.1, bf16[32,4096]{1,0:T(8,128)(2,1)} %bitcast.11, f32[1,4096]{1,0:T(1,128)} %bitcast.12, ...), custom_call_target="tpu_custom_call" | custom-call | tf_op jit(solution)/shard_map/pallas_call | solution.py:533
  60.8 47.8 %shard_map.132 = (bf16[128,4096]{1,0:T(8,128)(2,1)}, bf16[320,768]{1,0:T(8,128)(2,1)}) custom-call(bf16[128,4096]{1,0:T(8,128)(2,1)} %get-tuple-element.6.mixed_ref, bf16[320,768]{1,0:T(8,128)(2,1)} %get-tuple-element.7.hidden_ref), custom_call_target="tpu_custom_call" | custom-call | tf_op jit(solution)/shard_map/pallas_call | solution.py:581

commit v5 on v4

--- a/solution.py
+++ b/solution.py
@@ -480,17 +480,9 @@
         across_step(hop, sent, False)
 
 
-def hand_out(mixed_ref, hidden_ref, mixed_out, hidden_out, sems):
-    copies = []
-    for source, target in ((mixed_ref, mixed_out), (hidden_ref, hidden_out)):
-        share = source.shape[0] // 4
-        for part in range(4):
-            rows = pl.ds(part * share, share)
-            copies.append(pltpu.make_async_copy(source.at[rows, :], target.at[rows, :], sems.at[len(copies)]))
-    for copy in copies:
-        copy.start()
-    for copy in copies:
-        copy.wait()
+def hand_out(mixed_ref, hidden_ref, mixed_out, hidden_out):
+    mixed_out[...] = mixed_ref[...]
+    hidden_out[...] = hidden_ref[...]
 
 
 def shards(
@@ -578,15 +570,19 @@
             vmem_limit_bytes=VMEM_LIMIT, collective_id=0, has_side_effects=True
         ),
     )(*operands, gate_weight[0], up_weight[0])
+    strips = [
+        pl.BlockSpec((length // 4, channels), lambda turn: (turn, 0)),
+        pl.BlockSpec((slots // 4, hidden_rows), lambda turn: (turn, 0)),
+    ]
     mixed, hidden = pl.pallas_call(
         hand_out,
         out_shape=(
             jax.ShapeDtypeStruct((length, channels), half),
             jax.ShapeDtypeStruct((slots, hidden_rows), half),
         ),
-        in_specs=[in_hbm] * 2,
-        out_specs=(in_hbm, in_hbm),
-        scratch_shapes=[dma((8,))],
+        grid=(4,),
+        in_specs=strips,
+        out_specs=tuple(strips),
         compiler_params=pltpu.CompilerParams(vmem_limit_bytes=VMEM_LIMIT),
     )(mixed, hidden)
     return (mixed, hidden.T[None])

time: 109 us -> 64.6 us (0.59)
  Pallas kernels: 108 us -> 63.7 us
    pallas_call x1, Pallas kernels: 47.8 us -> 3.52 us  [shards(): pl.pallas_call(hand_out, out_shape=(jax.ShapeDtypeStruct((length, channel...]
where the time goes in v5:
time: 64.6 us; the launch traced here: 64.3 us
  Pallas kernels  63.7 us (99%)
    pallas_call x1, Pallas kernels, shards(): pl.pallas_call(functools.partial(mixer_kernel, count, flight), out_shape=...  60.2 us
    pallas_call x1, Pallas kernels, shards(): pl.pallas_call(hand_out, out_shape=(jax.ShapeDtypeStruct((length, channel...  3.52 us

profile of v5, /device:TPU:0, one launch (start us, length us, event | category | flops | bytes accessed | tf_op | source)
XLA Modules:
  0.0 64.3 jit_solution(9708617110741467122)
XLA Ops:
  0.6 60.2 %shard_map.131 = (bf16[128,4096]{1,0:T(8,128)(2,1)}, bf16[320,768]{1,0:T(8,128)(2,1)}) custom-call(bf16[128,4096]{1,0:T(8,128)(2,1)} %x_hbm.1, bf16[128,4096]{1,0:T(8,128)(2,1)} %z_hbm.1, bf16[128,4096]{1,0:T(8,128)(2,1)} %raw_hbm.1, f32[4,4096]{1,0:T(4,128)} %taps_hbm.1, bf16[32,4096]{1,0:T(8,128)(2,1)} %bitcast.11, f32[1,4096]{1,0:T(1,128)} %bitcast.12, ...), custom_call_target="tpu_custom_call" | custom-call | tf_op jit(solution)/shard_map/pallas_call | solution.py:525
  60.8 3.5 %shard_map.132 = (bf16[128,4096]{1,0:T(8,128)(2,1)}, bf16[320,768]{1,0:T(8,128)(2,1)}) custom-call(bf16[128,4096]{1,0:T(8,128)(2,1)} %get-tuple-element.6.mixed_ref, bf16[320,768]{1,0:T(8,128)(2,1)} %get-tuple-element.7.hidden_ref), custom_call_target="tpu_custom_call" | custom-call | tf_op jit(solution)/shard_map/pallas_call | solution.py:577
